TPU v7x, 256 devices: a whole 4x4x8 slice. The times are simulated.
256 devices in a mesh: space: 32 (over x, z_hi, core), sparse: 8 (over y, z_lo).
Axes of the slice: x: 4, y: 4, z: 8 (z_hi: 4, z_lo: 2; z = z_hi * 2 + z_lo), core: 2. Of those that a mesh axis runs over, the one named last changes fastest.
Arguments:
- positions: float32 [3, 8192], P(None, 'space'), may hold values from -4 to 4
- species: int32 [8192], P('space'), may hold values from 0 to 3
- live_count: int32 [32], P('space'), may hold values from 1 to 256, as said below
- neighbors: int32 [64, 8192], P(None, 'space'), may hold values from 0 to 511, as said below
- neighbor_mask: int32 [64, 8192], P(None, 'space'), may hold values from 0 to 1, as said below
- send_lo: int32 [4096], P('space'), may hold values from 0 to 255, as said below
- send_hi: int32 [4096], P('space'), may hold values from 0 to 255, as said below
- sparse_desc: bfloat16 [20480, 768], P('sparse'), may hold values from -6 to 6
- alpha: float32 [20480], P('sparse'), may hold values from -15 to 15
- var_factor: bfloat16 [20480, 128], P('sparse'), may hold values from -1.796875 to 1.796875
Outputs:
- forces: float32 [3, 8192], P(None, ('space', 'sparse'))
- energies: float32 [8192], P(('space', 'sparse'))
- variances: float32 [8192], P(('space', 'sparse'))
- virials: float32 [6, 8192], P(None, ('space', 'sparse'))
Inputs may be any that keep to these rules, and one draw needn't show every extreme that they name: The atoms present in brick b are its first live_count[b] slots; some brick holds 256. `neighbors`: indices into the brick's extended list: 256 own slots, then 128 ghosts from the brick below, then 128 from the brick above; an unmasked slot of a present atom names a present own atom or a ghost that exists. `neighbor_mask`: slot 0 of every present atom is used; atoms beyond the live count use no slot. `send_lo`: entries name present atoms of the sending brick, local to it. `send_hi`: entries name present atoms of the sending brick, local to it.
All inputs are finite; a program needn't handle non-finite values.
Results may differ from a plain program's by a relative error of at most 0.025.
Values may be sent and summed in bfloat16 or wider, within the bound.
A program may use at most 128 MiB of HBM per device.

v0:
```python
import jax
import jax.numpy as jnp
from jax import lax
from jax.experimental import pallas as pl
from jax.experimental.pallas import tpu as pltpu
from jax.sharding import PartitionSpec as P

EPS = 1e-6
F32, BF16 = jnp.float32, jnp.bfloat16
SPECIES, RADIAL = 4, 4
K = SPECIES * RADIAL
LANES = 128
RATES = tuple(scale * 2.0**r for scale in (0.1, 0.15) for r in range(RADIAL))
ORDERS = ((0, 1), (1, 4), (4, 10))
FOLD = (1.0,) * 7 + (2.0,) * 3
PAIRS = ((0, 0), (1, 1), (2, 2), (0, 1), (0, 2), (1, 2))
NT = (((1,), (1,)), ((), ()))


def angular(radial, o):
    first = [radial * o[p] for p in range(3)]
    return [radial] + first + [first[a] * o[b] for a, b in PAIRS]


def along(start, size):
    return pl.ds(pl.multiple_of(start, size), size)


def norms(sparse_ref, alpha_ref, scale_ref, chunk=512):
    count, depth = sparse_ref.shape
    ones = jnp.ones((8, depth), BF16)

    def step(t, _):
        raw = sparse_ref[along(t * chunk, chunk), :]
        squares = lax.dot_general(ones, raw * raw, NT, preferred_element_type=F32)
        inverse = 1.0 / (squares + EPS)
        alpha = alpha_ref[:, along(t * chunk, chunk)]
        row = lax.broadcasted_iota(jnp.int32, inverse.shape, 0)
        scale_ref[:, along(t * chunk, chunk)] = inverse * jnp.where(row == 0, 1.0, 2.0 * alpha)
        return 0

    lax.fori_loop(0, count // chunk, step, 0)


def pair_setup(table_ref, pos_ref, nb_ref, mask_ref, live, off_ref, w_ref, sp_ref, r_ref):
    own = pos_ref.shape[1]
    tables = table_ref.shape[1] // LANES
    blocks = nb_ref.shape[0] // 8
    lane = lax.broadcasted_iota(jnp.int32, (8, LANES), 1)

    def step(i, _):
        h, b = i // blocks, i % blocks
        rows, cols = along(b * 8, 8), along(h * LANES, LANES)
        index = nb_ref[rows, cols]
        low, high = index & (LANES - 1), index // LANES
        picked = []
        for c in range(4):
            value = None
            for t in range(tables):
                source = jnp.broadcast_to(table_ref[c : c + 1, t * LANES : (t + 1) * LANES], (8, LANES))
                part = jnp.take_along_axis(source, low, axis=1, mode="promise_in_bounds")
                value = part if value is None else jnp.where(high == t, part, value)
            picked.append(value)
        o = [picked[p] - pos_ref[p : p + 1, cols] for p in range(3)]
        alive = ((index >= own) | (index < live)) & (h * LANES + lane < live)
        valid = jnp.where(alive, mask_ref[rows, cols].astype(F32), 0.0)
        for p in range(3):
            off_ref[h, p, rows, :] = o[p]
        for s in range(SPECIES):
            w_ref[h, s, rows, :] = jnp.where(picked[3] == s, valid, 0.0)
        sp_ref[h, 0, rows, :] = picked[3]
        sp_ref[h, 1, rows, :] = valid
        square = o[0] * o[0] + o[1] * o[1] + o[2] * o[2]
        for e in range(2):
            radial = jnp.exp(square * (-RATES[e * RADIAL]))
            for r in range(RADIAL):
                if r:
                    radial = radial * radial
                r_ref[h, e * RADIAL + r, rows, :] = radial
        return 0

    lax.fori_loop(0, own // LANES * blocks, step, 0)


def moments(off_ref, w_ref, r_ref, acc_ref, m_ref, mc_ref):
    halves, _, count, _ = off_ref.shape
    rates = len(RATES)

    def step(i, _):
        h, er = i // rates, i % rates
        total = [[None] * 10 for _ in range(SPECIES)]
        for b in range(count // 8):
            rows = slice(b * 8, b * 8 + 8)
            v = angular(r_ref[h, er, rows, :], [off_ref[h, p, rows, :] for p in range(3)])
            for s in range(SPECIES):
                weight = w_ref[h, s, rows, :]
                for m in range(10):
                    term = weight * v[m]
                    total[s][m] = term if b == 0 else total[s][m] + term
        e, r = er // RADIAL, er % RADIAL
        for s in range(SPECIES):
            for m in range(10):
                acc_ref[(h * 2 + e) * 10 + m, along((s * RADIAL + r) * 8, 8), :] = total[s][m]
        return 0

    lax.fori_loop(0, halves * rates, step, 0)

    def fold(i, _):
        value = acc_ref[i, pl.ds(0, K, stride=8), :]
        for j in range(1, 8):
            value = value + acc_ref[i, pl.ds(j, K, stride=8), :]
        m_ref[i] = value
        mc_ref[i] = value * jnp.where(i % 10 >= 7, 2.0, 1.0)
        return 0

    lax.fori_loop(0, halves * 20, fold, 0)


def descriptors(m_ref, mc_ref, d_ref, rinv_ref, desc_ref, eye_ref):
    halves = d_ref.shape[0]
    for h in range(halves):
        base = h * 20

        def step(k, squares):
            for l, (start, stop) in enumerate(ORDERS):
                value = None
                for m in range(start, stop):
                    term = m_ref[base + m, pl.ds(k, 1), :] * mc_ref[base + 10 + m]
                    value = term if value is None else value + term
                d_ref[h, along(l * K * K + k * K, K), :] = value
                squares = squares + value * value
            return squares

        squares = lax.fori_loop(0, K, step, jnp.zeros((K, LANES), F32), unroll=2)
        rinv = lax.rsqrt(jnp.sum(squares, axis=0, keepdims=True) + EPS)
        rinv_ref[h] = jnp.broadcast_to(rinv, (8, LANES))
        unit = (d_ref[h] * rinv).astype(BF16)
        desc_ref[h * LANES : (h + 1) * LANES, :] = lax.dot_general(
            eye_ref[:LANES, :LANES], unit, NT, preferred_element_type=F32
        ).astype(BF16)


def kernel_sums(desc_ref, sparse_ref, scale_ref, factor_ref, grad_ref, vec_ref, energy_ref, chunk=512):
    count = sparse_ref.shape[0]
    for t in range(count // chunk):
        rows = slice(t * chunk, (t + 1) * chunk)
        raw = sparse_ref[rows, :]
        projection = lax.dot_general(desc_ref[...], raw, NT, preferred_element_type=F32)
        coefficient = projection * scale_ref[1:2, rows]
        kernel = projection * projection * scale_ref[0:1, rows]
        energy_terms = coefficient * projection
        energy = energy_terms[:, :LANES]
        for j in range(1, chunk // LANES):
            energy = energy + energy_terms[:, j * LANES : (j + 1) * LANES]
        grad = jnp.dot(coefficient.astype(BF16), raw, preferred_element_type=F32)
        vec = jnp.dot(kernel.astype(BF16), factor_ref[rows, :], preferred_element_type=F32)
        if t == 0:
            grad_ref[...] = grad
            vec_ref[...] = vec
            energy_ref[...] = energy
        else:
            grad_ref[...] += grad
            vec_ref[...] += vec
            energy_ref[...] += energy


def moment_grads(grad_ref, desc_ref, eye_ref, gd_ref, gt_ref, mc_ref, rinv_ref, g_ref):
    halves = gt_ref.shape[0]
    unit = desc_ref[...].astype(F32)
    grad = grad_ref[...]
    along_unit = jnp.sum(grad * unit, axis=1, keepdims=True)
    gd_ref[...] = (grad - unit * along_unit).astype(BF16)
    for h in range(halves):
        for l in range(3):
            gt_ref[h, l] = lax.dot_general(
                eye_ref[...],
                gd_ref[h * LANES : (h + 1) * LANES, l * K * K : (l + 1) * K * K],
                NT,
                preferred_element_type=F32,
            )

    def step(i, _):
        h, e = i // 2, i % 2
        rinv = rinv_ref[h, 0:1, :]
        for l, (start, stop) in enumerate(ORDERS):
            total = [None] * 10
            for j in range(K):
                block = gt_ref[h, l, along((1 - e) * K * K + j * K, K), :]
                for m in range(start, stop):
                    term = block * mc_ref[h * 20 + (1 - e) * 10 + m, j : j + 1, :]
                    total[m] = term if j == 0 else total[m] + term
            for m in range(start, stop):
                g_ref[i * 10 + m] = total[m] * rinv
        return 0

    lax.fori_loop(0, halves * 2, step, 0)


def pair_terms(off_ref, sp_ref, r_ref, g_ref, t_ref, own_ref, group=2):
    halves, _, count, _ = off_ref.shape
    blocks = count // 8 // group
    own_ref[...] = jnp.zeros(own_ref.shape, F32)
    for h in range(halves):
        t_ref[h, 9 * count :, :] = jnp.zeros((7 * count, LANES), F32)

    def step(i, _):
        h, b = i // blocks, i % blocks
        rows = [along((b * group + q) * 8, 8) for q in range(group)]
        o = [[off_ref[h, p, rows[q], :] for p in range(3)] for q in range(group)]
        ang = [[None] + o[q] + [o[q][x] * o[q][y] for x, y in PAIRS] for q in range(group)]
        kind = [sp_ref[h, 0, rows[q], :] for q in range(group)]
        hit = [[kind[q] == s for s in range(3)] for q in range(group)]
        top = [[None] * 10 for _ in range(group)]
        slope = [None] * group
        for er, rate in enumerate(RATES):
            e, r = er // RADIAL, er % RADIAL
            radial = [r_ref[h, er, rows[q], :] for q in range(group)]
            inner = [None] * group
            for m in range(10):
                g = [g_ref[(h * 2 + e) * 10 + m, s * RADIAL + r : s * RADIAL + r + 1, :] for s in range(SPECIES)]
                for q in range(group):
                    pick = jnp.where(hit[q][0], g[0], jnp.where(hit[q][1], g[1], jnp.where(hit[q][2], g[2], g[3])))
                    if m == 0:
                        inner[q] = pick
                    else:
                        inner[q] = inner[q] + pick * ang[q][m]
                        term = radial[q] * pick
                        top[q][m] = term if er == 0 else top[q][m] + term
            for q in range(group):
                term = (radial[q] * (-rate)) * inner[q]
                slope[q] = term if er == 0 else slope[q] + term
        sums = [None] * 9
        for q in range(group):
            x, y, z = o[q]
            t = top[q]
            valid = sp_ref[h, 1, rows[q], :]
            gx = valid * (t[1] + 2.0 * x * (t[4] + slope[q]) + t[7] * y + t[8] * z)
            gy = valid * (t[2] + 2.0 * y * (t[5] + slope[q]) + t[7] * x + t[9] * z)
            gz = valid * (t[3] + 2.0 * z * (t[6] + slope[q]) + t[8] * x + t[9] * y)
            g = [gx, gy, gz]
            terms = [-v for v in g] + [-0.5 * o[q][a] * g[c] for a, c in PAIRS]
            for c in range(9):
                t_ref[h, along(c * count + (b * group + q) * 8, 8), :] = terms[c]
                sums[c] = terms[c] if q == 0 else sums[c] + terms[c]
        for c in range(9):
            own_ref[h, c * 8 : c * 8 + 8, :] += -sums[c] if c < 3 else sums[c]
        return 0

    lax.fori_loop(0, halves * blocks, step, 0)


def scatter(nb_ref, t_ref, own_ref, energy_ref, tot_ref, unroll=4):
    count, own = nb_ref.shape
    halves = own // LANES
    tables = tot_ref.shape[0] // 16
    slot = lax.broadcasted_iota(jnp.int32, (LANES, own), 0)

    def step(i, total):
        left, right = [], []
        for u in range(unroll):
            n = i * unroll + u
            index = nb_ref[pl.ds(n, 1), :]
            low, high = index & (LANES - 1), index // LANES
            terms = jnp.concatenate([t_ref[h, pl.ds(n, 16, stride=count), :] for h in range(halves)], axis=1)
            left.append(
                jnp.concatenate([jnp.where(high == t, terms, 0.0) for t in range(tables)], axis=0).astype(BF16)
            )
            right.append(jnp.where(slot == low, 1.0, 0.0).astype(BF16))
        return total + lax.dot_general(
            jnp.concatenate(left, axis=1), jnp.concatenate(right, axis=1), NT, preferred_element_type=F32
        )

    total = lax.fori_loop(0, count // unroll, step, jnp.zeros(tot_ref.shape, F32))
    energies = 0.5 * lax.dot_general(
        jnp.ones((16, LANES), F32), energy_ref[...], NT, precision=lax.Precision.HIGHEST, preferred_element_type=F32
    )
    row = lax.broadcasted_iota(jnp.int32, (16, LANES), 0)
    for h in range(halves):
        mine = own_ref[h, pl.ds(0, 16, stride=8), :]
        for j in range(1, 8):
            mine = mine + own_ref[h, pl.ds(j, 16, stride=8), :]
        mine = jnp.where(row == 9, energies[:, h * LANES : (h + 1) * LANES], mine)
        tot_ref[h * 16 : (h + 1) * 16, :] = total[h * 16 : (h + 1) * 16, :] + mine
    for t in range(halves, tables):
        tot_ref[t * 16 : (t + 1) * 16, :] = total[t * 16 : (t + 1) * 16, :]


def identities(eye_ref):
    size = K * K
    row = lax.broadcasted_iota(jnp.int32, (size, size), 0)
    col = lax.broadcasted_iota(jnp.int32, (size, size), 1)
    eye_ref[:size, :] = jnp.where(row == col, 1.0, 0.0).astype(BF16)
    eye_ref[size:, :] = jnp.where((row % K) * K + row // K == col, 1.0, 0.0).astype(BF16)


def scratch_shapes(own, count, width, sparse, depth, rank):
    halves = own // LANES
    return dict(
        off=pltpu.VMEM((halves, 3, count, LANES), F32),
        w=pltpu.VMEM((halves, SPECIES, count, LANES), F32),
        sp=pltpu.VMEM((halves, 2, count, LANES), F32),
        r=pltpu.VMEM((halves, len(RATES), count, LANES), F32),
        acc=pltpu.VMEM((halves * 20, K * 8, LANES), F32),
        m=pltpu.VMEM((halves * 20, K, LANES), F32),
        mc=pltpu.VMEM((halves * 20, K, LANES), F32),
        d=pltpu.VMEM((halves, depth, LANES), F32),
        rinv=pltpu.VMEM((halves, 8, LANES), F32),
        desc=pltpu.VMEM((own, depth), BF16),
        eye=pltpu.VMEM((2 * K * K, K * K), BF16),
        scale=pltpu.VMEM((8, sparse), F32),
        grad=pltpu.VMEM((own, depth), F32),
        energy=pltpu.VMEM((own, LANES), F32),
        gd=pltpu.VMEM((own, depth), BF16),
        gt=pltpu.VMEM((halves, 3, 2 * K * K, LANES), F32),
        g=pltpu.VMEM((halves * 20, K, LANES), F32),
        t=pltpu.VMEM((halves, 16 * count, LANES), F32),
        own=pltpu.VMEM((halves, 16 * 8, LANES), F32),
    )


MESH = pl.DeviceIdType.MESH


def here():
    return lax.axis_index("space"), lax.axis_index("sparse"), lax.axis_size("space"), lax.axis_size("sparse")


def sides():
    brick, part, bricks, _ = here()
    return lax.rem(brick + bricks - 1, bricks), lax.rem(brick + 1, bricks)


def meet(peers):
    barrier = pltpu.get_barrier_semaphore()
    for peer in peers:
        pl.semaphore_signal(barrier, inc=1, device_id=peer, device_id_type=MESH)
    pl.semaphore_wait(barrier, len(peers))


def halo_peers():
    below, above = sides()
    part = lax.axis_index("sparse")
    return [(below, part), (above, part)]


def all_peers():
    brick, part, _, parts = here()
    below, above = sides()
    others = [lax.rem(part + j, parts) for j in range(parts)]
    return [(brick, o) for o in others[1:]] + [(side, o) for side in (below, above) for o in others]


def halo_pick(pos_ref, species_ref, send_refs, table_ref, face_ref):
    own = pos_ref.shape[1]
    table_ref[0:3, :own] = pos_ref[...]
    table_ref[3:4, :own] = species_ref[...].astype(F32)
    table_ref[4:8, :own] = jnp.zeros((4, own), F32)
    for f, send_ref in enumerate(send_refs):
        index = jnp.broadcast_to(send_ref[...], (8, LANES))
        low, high = index & (LANES - 1), index // LANES
        value = None
        for t in range(own // LANES):
            part = jnp.take_along_axis(
                table_ref[:, t * LANES : (t + 1) * LANES], low, axis=1, mode="promise_in_bounds"
            )
            value = part if value is None else jnp.where(high == t, part, value)
        face_ref[f] = value


def halo_copies(face_ref, rim_ref, send_sem, recv_sem):
    return [
        pltpu.make_async_remote_copy(
            src_ref=face_ref.at[f],
            dst_ref=rim_ref.at[1 - f],
            send_sem=send_sem.at[f],
            recv_sem=recv_sem.at[1 - f],
            device_id=peer,
            device_id_type=MESH,
        )
        for f, peer in enumerate(halo_peers())
    ]


def halo_place(rim_ref, table_ref, own):
    brick, _, bricks, _ = here()
    exists = (brick > 0, brick < bricks - 1)
    for f in range(2):
        table_ref[:, own + f * LANES : own + (f + 1) * LANES] = rim_ref[f] * jnp.where(exists[f], 1.0, 0.0)


def pack_messages(tot_ref, vec_ref, msg_ref, ghost_ref):
    own = vec_ref.shape[0]
    parts = msg_ref.shape[0]
    share = own // parts
    halves = own // LANES
    for p in range(parts):
        h = p * share // LANES
        msg_ref[p, :16, :] = tot_ref[h * 16 : (h + 1) * 16, :].astype(BF16)
        msg_ref[p, 16:, :] = vec_ref[p * share : (p + 1) * share, :].astype(BF16)
    for f in range(2):
        ghost_ref[f] = tot_ref[(halves + f) * 16 : (halves + f + 1) * 16, :].astype(BF16)


def message_copies(msg_ref, ghost_ref, msg_in, ghost_in, msg_sems, ghost_sems):
    brick, part, _, parts = here()
    copies = []
    for j in range(1, parts):
        other = lax.rem(part + j, parts)
        copies.append(
            pltpu.make_async_remote_copy(
                src_ref=msg_ref.at[other],
                dst_ref=msg_in.at[j],
                send_sem=msg_sems.at[0, j],
                recv_sem=msg_sems.at[1, j],
                device_id=(brick, other),
                device_id_type=MESH,
            )
        )
    for j in range(parts):
        other = lax.rem(part + j, parts)
        for f, side in enumerate(sides()):
            copies.append(
                pltpu.make_async_remote_copy(
                    src_ref=ghost_ref.at[f],
                    dst_ref=ghost_in.at[f, j],
                    send_sem=ghost_sems.at[0, f, j],
                    recv_sem=ghost_sems.at[1, f, j],
                    device_id=(side, other),
                    device_id_type=MESH,
                )
            )
    return copies


def finish(msg_ref, msg_in, ghost_in, send_refs, force_ref, energy_out, variance_ref, virial_ref):
    brick, part, bricks, parts = here()
    share = msg_ref.shape[1] - 16
    total = msg_ref[part].astype(F32)
    for j in range(1, parts):
        total = total + msg_in[j].astype(F32)
    mine, vec = total[:16], total[16:]
    half = part * share // LANES
    slot = half * LANES + lax.broadcasted_iota(jnp.int32, (LANES, LANES), 0)
    exists = (brick < bricks - 1, brick > 0)
    for f in range(2):
        ghosts = ghost_in[f, 0].astype(F32)
        for j in range(1, parts):
            ghosts = ghosts + ghost_in[f, j].astype(F32)
        ghosts = jnp.where(exists[f], ghosts, 0.0)
        hits = jnp.where(slot == send_refs[1 - f][...], 1.0, 0.0)
        high = ghosts.astype(BF16)
        low = (ghosts - high.astype(F32)).astype(BF16)
        both = lax.dot_general(
            jnp.concatenate([high, low], axis=0), hits.astype(BF16), NT, preferred_element_type=F32
        )
        row = lax.broadcasted_iota(jnp.int32, (16, LANES), 0)
        mine = mine + jnp.where(row < 9, both[:16] + both[16:], 0.0)
    shift = lax.rem(LANES - lax.rem(part * share, LANES), LANES)
    mine = pltpu.roll(mine, shift, 1)[:, :share]
    force_ref[...] = mine[0:3]
    virial_ref[...] = mine[3:9]
    energy_out[...] = mine[9:10]
    squares = lax.dot_general(
        jnp.ones((8, vec.shape[1]), F32), vec * vec, NT, precision=lax.Precision.HIGHEST, preferred_element_type=F32
    )
    variance_ref[...] = squares[0:1]

VM = pl.BlockSpec(memory_space=pltpu.VMEM)


def halo(pos, species, send_lo, send_hi):
    own = pos.shape[1]

    def kernel(pos_ref, species_ref, lo_ref, hi_ref, table_ref, face_ref, rim_ref, send_sem, recv_sem):
        halo_pick(pos_ref, species_ref, (lo_ref, hi_ref), table_ref, face_ref)
        meet(halo_peers())
        copies = halo_copies(face_ref, rim_ref, send_sem, recv_sem)
        for copy in copies:
            copy.start()
        for copy in copies:
            copy.wait()
        halo_place(rim_ref, table_ref, own)

    return pl.pallas_call(
        kernel,
        out_shape=jax.ShapeDtypeStruct((8, own + 2 * LANES), F32),
        in_specs=[VM] * 4,
        out_specs=VM,
        scratch_shapes=[
            pltpu.VMEM((2, 8, LANES), F32),
            pltpu.VMEM((2, 8, LANES), F32),
            pltpu.SemaphoreType.DMA((2,)),
            pltpu.SemaphoreType.DMA((2,)),
        ],
        compiler_params=pltpu.CompilerParams(collective_id=0, has_side_effects=True),
        name="halo",
    )(pos, species, send_lo, send_hi)


def brick(pos, nb, mask, live, table, sparse, alpha, factor):
    own, count, width = pos.shape[1], nb.shape[0], table.shape[1]
    names = scratch_shapes(own, count, width, sparse.shape[0], sparse.shape[1], factor.shape[1])
    keys = list(names)

    def kernel(
        live_ref, pos_ref, nb_ref, mask_ref, table_ref, sparse_ref, alpha_ref, factor_ref, tot_ref, vec_ref, *scratch
    ):
        s = dict(zip(keys, scratch))
        identities(s["eye"])
        norms(sparse_ref, alpha_ref, s["scale"])
        pair_setup(table_ref, pos_ref, nb_ref, mask_ref, live_ref[0], s["off"], s["w"], s["sp"], s["r"])
        moments(s["off"], s["w"], s["r"], s["acc"], s["m"], s["mc"])
        descriptors(s["m"], s["mc"], s["d"], s["rinv"], s["desc"], s["eye"])
        kernel_sums(s["desc"], sparse_ref, s["scale"], factor_ref, s["grad"], vec_ref, s["energy"])
        moment_grads(s["grad"], s["desc"], s["eye"], s["gd"], s["gt"], s["mc"], s["rinv"], s["g"])
        pair_terms(s["off"], s["sp"], s["r"], s["g"], s["t"], s["own"])
        scatter(nb_ref, s["t"], s["own"], s["energy"], tot_ref)

    return pl.pallas_call(
        kernel,
        out_shape=(
            jax.ShapeDtypeStruct((width // LANES * 16, LANES), F32),
            jax.ShapeDtypeStruct((own, factor.shape[1]), F32),
        ),
        in_specs=[pl.BlockSpec(memory_space=pltpu.SMEM)] + [VM] * 7,
        out_specs=(VM, VM),
        scratch_shapes=list(names.values()),
        compiler_params=pltpu.CompilerParams(vmem_limit_bytes=60 * 1024 * 1024),
        name="brick",
    )(live, pos, nb, mask, table, sparse, alpha, factor)


def exchange(tot, vec, send_lo, send_hi, parts):
    own, rank = vec.shape
    share = own // parts
    slots = lambda *lead: pltpu.VMEM((*lead, 16 + share, rank), BF16)
    faces = lambda *lead: pltpu.VMEM((*lead, 16, LANES), BF16)

    def kernel(
        tot_ref, vec_ref, lo_ref, hi_ref, force_ref, energy_ref, variance_ref, virial_ref, msg, ghost, msg_in, ghost_in, msg_sems, ghost_sems
    ):
        pack_messages(tot_ref, vec_ref, msg, ghost)
        meet(all_peers())
        copies = message_copies(msg, ghost, msg_in, ghost_in, msg_sems, ghost_sems)
        for copy in copies:
            copy.start()
        for copy in copies:
            copy.wait()
        finish(msg, msg_in, ghost_in, (lo_ref, hi_ref), force_ref, energy_ref, variance_ref, virial_ref)

    return pl.pallas_call(
        kernel,
        out_shape=tuple(jax.ShapeDtypeStruct((n, share), F32) for n in (3, 1, 1, 6)),
        in_specs=[VM] * 4,
        out_specs=(VM,) * 4,
        scratch_shapes=[
            slots(parts),
            faces(2),
            slots(parts),
            faces(2, parts),
            pltpu.SemaphoreType.DMA((2, parts)),
            pltpu.SemaphoreType.DMA((2, 2, parts)),
        ],
        compiler_params=pltpu.CompilerParams(collective_id=1, has_side_effects=True),
        name="exchange",
    )(tot, vec, send_lo, send_hi)


def shards(
    positions, species, live_count, neighbors, neighbor_mask, send_lo, send_hi, sparse_desc, alpha, var_factor
):
    lo, hi = send_lo[None], send_hi[None]
    table = halo(positions, species[None], lo, hi)
    tot, vec = brick(positions, neighbors, neighbor_mask, live_count, table, sparse_desc, alpha[None], var_factor)
    forces, energies, variances, virials = exchange(tot, vec, lo, hi, lax.axis_size("sparse"))
    return forces, energies[0], variances[0], virials


def solution(mesh):
    return jax.shard_map(
        shards,
        mesh=mesh,
        in_specs=(
            P(None, "space"),
            P("space"),
            P("space"),
            P(None, "space"),
            P(None, "space"),
            P("space"),
            P("space"),
            P("sparse", None),
            P("sparse"),
            P("sparse", None),
        ),
        out_specs=(
            P(None, ("space", "sparse")),
            P(("space", "sparse")),
            P(("space", "sparse")),
            P(None, ("space", "sparse")),
        ),
        check_vma=False,
    )
```

profile of v0, /device:TPU:1, one launch (start us, length us, event | category | flops | bytes accessed | tf_op | source)
XLA Modules:
  0.0 53.4 jit_solution(9132458859452867417)
XLA Ops:
  1.3 1.3 %broadcast_in_dim.15.alpha_ref = f32[1,2560]{1,0:T(1,128)} reshape(f32[2560]{0:T(1024)} %param.18) | data formatting | bytes 20480 | tf_op jit(solution)/shard_map/broadcast_in_dim | solution.py:574
  2.6 11.5 %halo.1.table_ref = f32[8,512]{1,0:T(8,128)} custom-call(f32[3,256]{1,0:T(4,128)} %pos_ref.3, s32[1,256]{1,0:T(1,128)} %bitcast.9, s32[1,128]{1,0:T(1,128)} %bitcast.5, s32[1,128]{1,0:T(1,128)} %bitcast.7), custom_call_target="tpu_custom_call" | custom-call | tf_op jit(solution)/shard_map/halo/pallas_call | solution.py:484
  14.1 18.8 %brick.1 = (f32[64,128]{1,0:T(8,128)}, f32[256,128]{1,0:T(8,128)}) custom-call(s32[1]{0:T(128)S(6)} %copy.18.live_ref, f32[3,256]{1,0:T(4,128)} %pos_ref.3, s32[64,256]{1,0:T(8,128)} %nb_ref.1, s32[64,256]{1,0:T(8,128)} %mask_ref.1, f32[8,512]{1,0:T(8,128)} %halo.1.table_ref, bf16[2560,768]{1,0:T(8,128)(2,1)} %sparse_ref.1, ...), custom_call_target="tpu_custom_call" | custom-call | tf_op jit(solution)/shard_map/brick/pallas_call | solution.py:519
  32.9 15.8 %exchange.1 = (f32[3,32]{1,0:T(4,128)}, f32[1,32]{1,0:T(1,128)}, f32[1,32]{1,0:T(1,128)}, f32[6,32]{1,0:T(8,128)}) custom-call(f32[64,128]{1,0:T(8,128)} %get-tuple-element.10.tot_ref, f32[256,128]{1,0:T(8,128)} %get-tuple-element.11.vec_ref, s32[1,128]{1,0:T(1,128)} %bitcast.6, s32[1,128]{1,0:T(1,128)} %bitcast.8), custom_call_target="tpu_custom_call" | custom-call | tf_op jit(solution)/shard_map/exchange/pallas_call | solution.py:551
  48.6 1.2 %copy.19 = f32[3,32]{1,0:T(4,128)} copy(f32[3,32]{1,0:T(4,128)} %get-tuple-element.20) | data formatting | bytes 768
  49.9 1.1 %copy.20 = f32[32]{0:T(128)} copy(f32[32]{0:T(128)} %bitcast.11) | data formatting | bytes 256
  51.0 1.1 %copy.21 = f32[32]{0:T(128)} copy(f32[32]{0:T(128)} %bitcast.10) | data formatting | bytes 256
  52.1 1.3 %copy.22 = f32[6,32]{1,0:T(8,128)} copy(f32[6,32]{1,0:T(8,128)} %get-tuple-element.23) | data formatting | bytes 1536
where the time goes:
time: 53.7 us; the launch traced here: 53.4 us
  Pallas kernels  46 us (86%)
  local copies, waits for them, and re-layouts  6.07 us (11%)
  between operations  1.3 us (2%)
    pallas_call x1, Pallas kernels, brick(): pl.pallas_call(kernel, out_shape=(jax.ShapeDtypeStruct((width // LANES *...  18.8 us
    pallas_call x1, Pallas kernels, exchange(): pl.pallas_call(kernel, out_shape=tuple((jax.ShapeDtypeStruct((n, share),...  15.8 us
    pallas_call x1, Pallas kernels, halo(): pl.pallas_call(kernel, out_shape=jax.ShapeDtypeStruct((8, own + 2 * LANES...  11.5 us
    unnamed x4, local copies, waits for them, and re-layouts  4.76 us
    broadcast_in_dim x1, local copies, waits for them, and re-layouts, shards(): alpha[None]  1.31 us

commit v1 on v0

--- a/solution.py
+++ b/solution.py
@@ -26,20 +26,17 @@
     return pl.ds(pl.multiple_of(start, size), size)
 
 
-def norms(sparse_ref, alpha_ref, scale_ref, chunk=512):
-    count, depth = sparse_ref.shape
+def norms(sparse_ref, alpha_ref, scale_ref, first, last, chunk=512):
+    depth = sparse_ref.shape[1]
     ones = jnp.ones((8, depth), BF16)
-
-    def step(t, _):
-        raw = sparse_ref[along(t * chunk, chunk), :]
+    row = lax.broadcasted_iota(jnp.int32, (8, chunk), 0)
+    for t in range(first, last):
+        raw = sparse_ref[t * chunk : (t + 1) * chunk, :]
         squares = lax.dot_general(ones, raw * raw, NT, preferred_element_type=F32)
         inverse = 1.0 / (squares + EPS)
-        alpha = alpha_ref[:, along(t * chunk, chunk)]
-        row = lax.broadcasted_iota(jnp.int32, inverse.shape, 0)
-        scale_ref[:, along(t * chunk, chunk)] = inverse * jnp.where(row == 0, 1.0, 2.0 * alpha)
-        return 0
-
-    lax.fori_loop(0, count // chunk, step, 0)
+        per = chunk // LANES
+        alpha = jnp.concatenate([alpha_ref[t * per + j : t * per + j + 1, :] for j in range(per)], axis=1)
+        scale_ref[:, t * chunk : (t + 1) * chunk] = inverse * jnp.where(row == 0, 1.0, 2.0 * alpha)
 
 
 def pair_setup(table_ref, pos_ref, nb_ref, mask_ref, live, off_ref, w_ref, sp_ref, r_ref):
@@ -330,13 +327,6 @@
     return lax.rem(brick + bricks - 1, bricks), lax.rem(brick + 1, bricks)
 
 
-def meet(peers):
-    barrier = pltpu.get_barrier_semaphore()
-    for peer in peers:
-        pl.semaphore_signal(barrier, inc=1, device_id=peer, device_id_type=MESH)
-    pl.semaphore_wait(barrier, len(peers))
-
-
 def halo_peers():
     below, above = sides()
     part = lax.axis_index("sparse")
@@ -432,7 +422,7 @@
     return copies
 
 
-def finish(msg_ref, msg_in, ghost_in, send_refs, force_ref, energy_out, variance_ref, virial_ref):
+def finish(msg_ref, msg_in, ghost_in, send_refs, out_ref):
     brick, part, bricks, parts = here()
     share = msg_ref.shape[1] - 16
     total = msg_ref[part].astype(F32)
@@ -456,123 +446,132 @@
         row = lax.broadcasted_iota(jnp.int32, (16, LANES), 0)
         mine = mine + jnp.where(row < 9, both[:16] + both[16:], 0.0)
     shift = lax.rem(LANES - lax.rem(part * share, LANES), LANES)
-    mine = pltpu.roll(mine, shift, 1)[:, :share]
-    force_ref[...] = mine[0:3]
-    virial_ref[...] = mine[3:9]
-    energy_out[...] = mine[9:10]
+    mine = pltpu.roll(mine, shift, 1)
     squares = lax.dot_general(
-        jnp.ones((8, vec.shape[1]), F32), vec * vec, NT, precision=lax.Precision.HIGHEST, preferred_element_type=F32
+        jnp.ones((16, vec.shape[1]), F32), vec * vec, NT, precision=lax.Precision.HIGHEST, preferred_element_type=F32
     )
-    variance_ref[...] = squares[0:1]
+    out_ref[...] = mine
+    out_ref[10:11, :share] = squares[10:11]
 
 VM = pl.BlockSpec(memory_space=pltpu.VMEM)
-
-
-def halo(pos, species, send_lo, send_hi):
-    own = pos.shape[1]
-
-    def kernel(pos_ref, species_ref, lo_ref, hi_ref, table_ref, face_ref, rim_ref, send_sem, recv_sem):
-        halo_pick(pos_ref, species_ref, (lo_ref, hi_ref), table_ref, face_ref)
-        meet(halo_peers())
-        copies = halo_copies(face_ref, rim_ref, send_sem, recv_sem)
+HBM = pl.BlockSpec(memory_space=pl.ANY)
+
+
+def brick(pos, species, live, nb, mask, send_lo, send_hi, sparse, alpha, factor, parts):
+    own, count = pos.shape[1], nb.shape[0]
+    depth, rank = sparse.shape[1], factor.shape[1]
+    tables = own // LANES + 2
+    share = own // parts
+    names = scratch_shapes(own, count, tables * LANES, sparse.shape[0], depth, rank)
+    names.update(
+        table=pltpu.VMEM((8, tables * LANES), F32),
+        face=pltpu.VMEM((2, 8, LANES), F32),
+        rim=pltpu.VMEM((2, 8, LANES), F32),
+        sparse=pltpu.VMEM(sparse.shape, BF16),
+        factor=pltpu.VMEM(factor.shape, BF16),
+        vec=pltpu.VMEM((own, rank), F32),
+        tot=pltpu.VMEM((tables * 16, LANES), F32),
+        msg=pltpu.VMEM((parts, 16 + share, rank), BF16),
+        msg_in=pltpu.VMEM((parts, 16 + share, rank), BF16),
+        ghost=pltpu.VMEM((2, 16, LANES), BF16),
+        ghost_in=pltpu.VMEM((2, parts, 16, LANES), BF16),
+        halo_send=pltpu.SemaphoreType.DMA((2,)),
+        halo_recv=pltpu.SemaphoreType.DMA((2,)),
+        msg_sems=pltpu.SemaphoreType.DMA((2, parts)),
+        ghost_sems=pltpu.SemaphoreType.DMA((2, 2, parts)),
+        load_sems=pltpu.SemaphoreType.DMA((2,)),
+    )
+    keys = list(names)
+
+    def kernel(
+        live_ref, pos_ref, species_ref, nb_ref, mask_ref, lo_ref, hi_ref, alpha_ref, sparse_hbm, factor_hbm, out_ref, *scratch
+    ):
+        s = dict(zip(keys, scratch))
+        peers = all_peers()
+        barrier = pltpu.get_barrier_semaphore()
+        for peer in peers:
+            pl.semaphore_signal(barrier, inc=1, device_id=peer, device_id_type=MESH)
+        loads = [
+            pltpu.make_async_copy(sparse_hbm, s["sparse"], s["load_sems"].at[0]),
+            pltpu.make_async_copy(factor_hbm, s["factor"], s["load_sems"].at[1]),
+        ]
+        for load in loads:
+            load.start()
+        halo_pick(pos_ref, species_ref, (lo_ref, hi_ref), s["table"], s["face"])
+        identities(s["eye"])
+        for load in loads:
+            load.wait()
+        norms(s["sparse"], alpha_ref, s["scale"], 0, 2)
+        pl.semaphore_wait(barrier, len(peers))
+        halos = halo_copies(s["face"], s["rim"], s["halo_send"], s["halo_recv"])
+        for copy in halos:
+            copy.start()
+        norms(s["sparse"], alpha_ref, s["scale"], 2, sparse.shape[0] // 512)
+        for copy in halos:
+            copy.wait()
+        halo_place(s["rim"], s["table"], own)
+        pair_setup(s["table"], pos_ref, nb_ref, mask_ref, live_ref[0], s["off"], s["w"], s["sp"], s["r"])
+        moments(s["off"], s["w"], s["r"], s["acc"], s["m"], s["mc"])
+        descriptors(s["m"], s["mc"], s["d"], s["rinv"], s["desc"], s["eye"])
+        kernel_sums(s["desc"], s["sparse"], s["scale"], s["factor"], s["grad"], s["vec"], s["energy"])
+        moment_grads(s["grad"], s["desc"], s["eye"], s["gd"], s["gt"], s["mc"], s["rinv"], s["g"])
+        pair_terms(s["off"], s["sp"], s["r"], s["g"], s["t"], s["own"])
+        scatter(nb_ref, s["t"], s["own"], s["energy"], s["tot"])
+        pack_messages(s["tot"], s["vec"], s["msg"], s["ghost"])
+        copies = message_copies(s["msg"], s["ghost"], s["msg_in"], s["ghost_in"], s["msg_sems"], s["ghost_sems"])
         for copy in copies:
             copy.start()
         for copy in copies:
             copy.wait()
-        halo_place(rim_ref, table_ref, own)
+        finish(s["msg"], s["msg_in"], s["ghost_in"], (lo_ref, hi_ref), out_ref)
 
     return pl.pallas_call(
         kernel,
-        out_shape=jax.ShapeDtypeStruct((8, own + 2 * LANES), F32),
-        in_specs=[VM] * 4,
+        out_shape=jax.ShapeDtypeStruct((16, LANES), F32),
+        in_specs=[pl.BlockSpec(memory_space=pltpu.SMEM)] + [VM] * 7 + [HBM] * 2,
         out_specs=VM,
-        scratch_shapes=[
-            pltpu.VMEM((2, 8, LANES), F32),
-            pltpu.VMEM((2, 8, LANES), F32),
-            pltpu.SemaphoreType.DMA((2,)),
-            pltpu.SemaphoreType.DMA((2,)),
-        ],
-        compiler_params=pltpu.CompilerParams(collective_id=0, has_side_effects=True),
-        name="halo",
-    )(pos, species, send_lo, send_hi)
-
-
-def brick(pos, nb, mask, live, table, sparse, alpha, factor):
-    own, count, width = pos.shape[1], nb.shape[0], table.shape[1]
-    names = scratch_shapes(own, count, width, sparse.shape[0], sparse.shape[1], factor.shape[1])
-    keys = list(names)
-
-    def kernel(
-        live_ref, pos_ref, nb_ref, mask_ref, table_ref, sparse_ref, alpha_ref, factor_ref, tot_ref, vec_ref, *scratch
-    ):
-        s = dict(zip(keys, scratch))
-        identities(s["eye"])
-        norms(sparse_ref, alpha_ref, s["scale"])
-        pair_setup(table_ref, pos_ref, nb_ref, mask_ref, live_ref[0], s["off"], s["w"], s["sp"], s["r"])
-        moments(s["off"], s["w"], s["r"], s["acc"], s["m"], s["mc"])
-        descriptors(s["m"], s["mc"], s["d"], s["rinv"], s["desc"], s["eye"])
-        kernel_sums(s["desc"], sparse_ref, s["scale"], factor_ref, s["grad"], vec_ref, s["energy"])
-        moment_grads(s["grad"], s["desc"], s["eye"], s["gd"], s["gt"], s["mc"], s["rinv"], s["g"])
-        pair_terms(s["off"], s["sp"], s["r"], s["g"], s["t"], s["own"])
-        scatter(nb_ref, s["t"], s["own"], s["energy"], tot_ref)
-
-    return pl.pallas_call(
-        kernel,
-        out_shape=(
-            jax.ShapeDtypeStruct((width // LANES * 16, LANES), F32),
-            jax.ShapeDtypeStruct((own, factor.shape[1]), F32),
+        scratch_shapes=list(names.values()),
+        compiler_params=pltpu.CompilerParams(
+            vmem_limit_bytes=60 * 1024 * 1024, collective_id=0, has_side_effects=True
         ),
-        in_specs=[pl.BlockSpec(memory_space=pltpu.SMEM)] + [VM] * 7,
-        out_specs=(VM, VM),
-        scratch_shapes=list(names.values()),
-        compiler_params=pltpu.CompilerParams(vmem_limit_bytes=60 * 1024 * 1024),
         name="brick",
-    )(live, pos, nb, mask, table, sparse, alpha, factor)
-
-
-def exchange(tot, vec, send_lo, send_hi, parts):
-    own, rank = vec.shape
-    share = own // parts
-    slots = lambda *lead: pltpu.VMEM((*lead, 16 + share, rank), BF16)
-    faces = lambda *lead: pltpu.VMEM((*lead, 16, LANES), BF16)
-
-    def kernel(
-        tot_ref, vec_ref, lo_ref, hi_ref, force_ref, energy_ref, variance_ref, virial_ref, msg, ghost, msg_in, ghost_in, msg_sems, ghost_sems
-    ):
-        pack_messages(tot_ref, vec_ref, msg, ghost)
-        meet(all_peers())
-        copies = message_copies(msg, ghost, msg_in, ghost_in, msg_sems, ghost_sems)
-        for copy in copies:
-            copy.start()
-        for copy in copies:
-            copy.wait()
-        finish(msg, msg_in, ghost_in, (lo_ref, hi_ref), force_ref, energy_ref, variance_ref, virial_ref)
+    )(live, pos, species, nb, mask, send_lo, send_hi, alpha, sparse, factor)
+
+
+def split(result, share):
+    def kernel(result_ref, force_ref, energy_ref, variance_ref, virial_ref):
+        force_ref[...] = result_ref[0:3, :share]
+        virial_ref[...] = result_ref[3:9, :share]
+        energy_ref[...] = result_ref[9:10, :share]
+        variance_ref[...] = result_ref[10:11, :share]
 
     return pl.pallas_call(
         kernel,
         out_shape=tuple(jax.ShapeDtypeStruct((n, share), F32) for n in (3, 1, 1, 6)),
-        in_specs=[VM] * 4,
+        in_specs=[VM],
         out_specs=(VM,) * 4,
-        scratch_shapes=[
-            slots(parts),
-            faces(2),
-            slots(parts),
-            faces(2, parts),
-            pltpu.SemaphoreType.DMA((2, parts)),
-            pltpu.SemaphoreType.DMA((2, 2, parts)),
-        ],
-        compiler_params=pltpu.CompilerParams(collective_id=1, has_side_effects=True),
-        name="exchange",
-    )(tot, vec, send_lo, send_hi)
+        name="split",
+    )(result)
 
 
 def shards(
     positions, species, live_count, neighbors, neighbor_mask, send_lo, send_hi, sparse_desc, alpha, var_factor
 ):
-    lo, hi = send_lo[None], send_hi[None]
-    table = halo(positions, species[None], lo, hi)
-    tot, vec = brick(positions, neighbors, neighbor_mask, live_count, table, sparse_desc, alpha[None], var_factor)
-    forces, energies, variances, virials = exchange(tot, vec, lo, hi, lax.axis_size("sparse"))
+    parts = lax.axis_size("sparse")
+    result = brick(
+        positions,
+        species[None],
+        live_count,
+        neighbors,
+        neighbor_mask,
+        send_lo[None],
+        send_hi[None],
+        sparse_desc,
+        alpha.reshape(-1, LANES),
+        var_factor,
+        parts,
+    )
+    forces, energies, variances, virials = split(result, positions.shape[1] // parts)
     return forces, energies[0], variances[0], virials
 
 

time: 53.7 us -> 39.7 us (0.74)
  the two profiles are of different devices: /device:TPU:1 before, /device:TPU:32 now
where the time goes in v1:
time: 39.7 us; the launch traced here: 39.5 us
  Pallas kernels  38.3 us (96%)
  between operations  1.29 us (3%)
    pallas_call x1, Pallas kernels, brick(): pl.pallas_call(kernel, out_shape=jax.ShapeDtypeStruct((16, LANES), F32),...  37 us
    pallas_call x1, Pallas kernels, split(): pl.pallas_call(kernel, out_shape=tuple((jax.ShapeDtypeStruct((n, share),...  1.3 us

profile of v1, /device:TPU:32, one launch (start us, length us, event | category | flops | bytes accessed | tf_op | source)
XLA Modules:
  0.0 39.5 jit_solution(11264047449882367978)
XLA Ops:
  1.3 37.0 %brick.1.result_ref = f32[16,128]{1,0:T(8,128)} custom-call(s32[1]{0:T(128)S(6)} %copy.14.live_ref, f32[3,256]{1,0:T(4,128)} %pos_ref.1, s32[1,256]{1,0:T(1,128)} %bitcast.7, s32[64,256]{1,0:T(8,128)} %nb_ref.1, s32[64,256]{1,0:T(8,128)} %mask_ref.1, s32[1,128]{1,0:T(1,128)} %bitcast.8, s32[1,128]{1,0:T(1,128)} %bitcast.9, f32[20,128]{1,0:T(8,128)} %bitcast.6, ...), custom_call_target="tpu_custom_call" | custom-call | tf_op jit(solution)/shard_map/brick/pallas_call | solution.py:528
  38.2 1.3 %split.1 = (f32[3,32]{1,0:T(4,128)}, f32[1,32]{1,0:T(1,128)}, f32[1,32]{1,0:T(1,128)}, f32[6,32]{1,0:T(8,128)}) custom-call(f32[16,128]{1,0:T(8,128)} %brick.1.result_ref), custom_call_target="tpu_custom_call" | custom-call | tf_op jit(solution)/shard_map/split/pallas_call | solution.py:548

commit v2 on v1

--- a/solution.py
+++ b/solution.py
@@ -28,13 +28,17 @@
 
 def norms(sparse_ref, alpha_ref, scale_ref, first, last, chunk=512):
     depth = sparse_ref.shape[1]
-    ones = jnp.ones((8, depth), BF16)
+    ones = jnp.ones((8, LANES), BF16)
     row = lax.broadcasted_iota(jnp.int32, (8, chunk), 0)
+    per = chunk // LANES
     for t in range(first, last):
         raw = sparse_ref[t * chunk : (t + 1) * chunk, :]
-        squares = lax.dot_general(ones, raw * raw, NT, preferred_element_type=F32)
+        parts = [raw[:, j * LANES : (j + 1) * LANES] for j in range(depth // LANES)]
+        parts = [part * part for part in parts]
+        while len(parts) > 1:
+            parts = [x + y for x, y in zip(parts[::2], parts[1::2])] + parts[len(parts) // 2 * 2 :]
+        squares = lax.dot_general(ones, parts[0], NT, preferred_element_type=F32)
         inverse = 1.0 / (squares + EPS)
-        per = chunk // LANES
         alpha = jnp.concatenate([alpha_ref[t * per + j : t * per + j + 1, :] for j in range(per)], axis=1)
         scale_ref[:, t * chunk : (t + 1) * chunk] = inverse * jnp.where(row == 0, 1.0, 2.0 * alpha)
 
@@ -76,7 +80,7 @@
                 r_ref[h, e * RADIAL + r, rows, :] = radial
         return 0
 
-    lax.fori_loop(0, own // LANES * blocks, step, 0)
+    lax.fori_loop(0, own // LANES * blocks, step, 0, unroll=8)
 
 
 def moments(off_ref, w_ref, r_ref, acc_ref, m_ref, mc_ref):
@@ -110,7 +114,7 @@
         mc_ref[i] = value * jnp.where(i % 10 >= 7, 2.0, 1.0)
         return 0
 
-    lax.fori_loop(0, halves * 20, fold, 0)
+    lax.fori_loop(0, halves * 20, fold, 0, unroll=8)
 
 
 def descriptors(m_ref, mc_ref, d_ref, rinv_ref, desc_ref, eye_ref):
@@ -246,23 +250,29 @@
     lax.fori_loop(0, halves * blocks, step, 0)
 
 
-def scatter(nb_ref, t_ref, own_ref, energy_ref, tot_ref, unroll=4):
+def scatter(nb_ref, t_ref, own_ref, energy_ref, tot_ref, unroll=32):
     count, own = nb_ref.shape
     halves = own // LANES
     tables = tot_ref.shape[0] // 16
-    slot = lax.broadcasted_iota(jnp.int32, (LANES, own), 0)
+    slot = lax.broadcasted_iota(jnp.int32, (LANES, own), 0).astype(F32).astype(BF16)
 
     def step(i, total):
         left, right = [], []
         for u in range(unroll):
             n = i * unroll + u
-            index = nb_ref[pl.ds(n, 1), :]
-            low, high = index & (LANES - 1), index // LANES
-            terms = jnp.concatenate([t_ref[h, pl.ds(n, 16, stride=count), :] for h in range(halves)], axis=1)
-            left.append(
-                jnp.concatenate([jnp.where(high == t, terms, 0.0) for t in range(tables)], axis=0).astype(BF16)
+            index = jnp.broadcast_to(nb_ref[pl.ds(n, 1), :], (16, own))
+            low = (index & (LANES - 1)).astype(F32).astype(BF16)
+            high = (index // LANES).astype(F32).astype(BF16)
+            terms = jnp.concatenate(
+                [t_ref[h, pl.ds(n, 16, stride=count), :] for h in range(halves)], axis=1
+            ).astype(BF16)
+            zero, one = jnp.zeros_like(terms), jnp.ones_like(terms)
+            left.append(jnp.concatenate([jnp.where(high == t, terms, zero) for t in range(tables)], axis=0))
+            right.append(
+                jnp.concatenate(
+                    [jnp.where(slot[j : j + 16] == low, one, zero) for j in range(0, LANES, 16)], axis=0
+                )
             )
-            right.append(jnp.where(slot == low, 1.0, 0.0).astype(BF16))
         return total + lax.dot_general(
             jnp.concatenate(left, axis=1), jnp.concatenate(right, axis=1), NT, preferred_element_type=F32
         )
@@ -318,26 +328,46 @@
 MESH = pl.DeviceIdType.MESH
 
 
-def here():
-    return lax.axis_index("space"), lax.axis_index("sparse"), lax.axis_size("space"), lax.axis_size("sparse")
-
-
-def sides():
-    brick, part, bricks, _ = here()
-    return lax.rem(brick + bricks - 1, bricks), lax.rem(brick + 1, bricks)
-
-
-def halo_peers():
-    below, above = sides()
-    part = lax.axis_index("sparse")
-    return [(below, part), (above, part)]
-
-
-def all_peers():
-    brick, part, _, parts = here()
-    below, above = sides()
-    others = [lax.rem(part + j, parts) for j in range(parts)]
-    return [(brick, o) for o in others[1:]] + [(side, o) for side in (below, above) for o in others]
+def remote(source, target, sems, slot, device):
+    return pltpu.make_async_remote_copy(
+        src_ref=source,
+        dst_ref=target,
+        send_sem=sems.at[(0, *slot)],
+        recv_sem=sems.at[(1, *slot)],
+        device_id=device,
+        device_id_type=MESH,
+    )
+
+
+class Place:
+    def __init__(self):
+        self.brick, self.part = lax.axis_index("space"), lax.axis_index("sparse")
+        bricks, self.parts = lax.axis_size("space"), lax.axis_size("sparse")
+        self.odd = lax.rem(self.brick, 2)
+        self.mate = self.brick + 1 - 2 * self.odd
+        self.exists = (self.brick > 0) & (self.brick < bricks - 1)
+        self.cross = jnp.where(self.exists, self.brick - 1 + 2 * self.odd, self.mate)
+        self.others = [lax.rem(self.part + j, self.parts) for j in range(self.parts)]
+
+    def greet(self):
+        barrier = pltpu.get_barrier_semaphore()
+
+        def signal(device):
+            pl.semaphore_signal(barrier, inc=1, device_id=device, device_id_type=MESH)
+
+        signal((self.mate, self.part))
+
+        @pl.when(self.exists)
+        def _():
+            for other in self.others:
+                signal((self.cross, other))
+
+        for other in self.others[1:]:
+            signal((self.brick, other))
+
+    def met(self):
+        barrier = pltpu.get_barrier_semaphore()
+        pl.semaphore_wait(barrier, jnp.where(self.exists, 2 * self.parts, self.parts))
 
 
 def halo_pick(pos_ref, species_ref, send_refs, table_ref, face_ref):
@@ -357,185 +387,195 @@
         face_ref[f] = value
 
 
-def halo_copies(face_ref, rim_ref, send_sem, recv_sem):
-    return [
-        pltpu.make_async_remote_copy(
-            src_ref=face_ref.at[f],
-            dst_ref=rim_ref.at[1 - f],
-            send_sem=send_sem.at[f],
-            recv_sem=recv_sem.at[1 - f],
-            device_id=peer,
-            device_id_type=MESH,
-        )
-        for f, peer in enumerate(halo_peers())
-    ]
-
-
-def halo_place(rim_ref, table_ref, own):
-    brick, _, bricks, _ = here()
-    exists = (brick > 0, brick < bricks - 1)
-    for f in range(2):
-        table_ref[:, own + f * LANES : own + (f + 1) * LANES] = rim_ref[f] * jnp.where(exists[f], 1.0, 0.0)
-
-
-def pack_messages(tot_ref, vec_ref, msg_ref, ghost_ref):
-    own = vec_ref.shape[0]
-    parts = msg_ref.shape[0]
-    share = own // parts
-    halves = own // LANES
-    for p in range(parts):
-        h = p * share // LANES
-        msg_ref[p, :16, :] = tot_ref[h * 16 : (h + 1) * 16, :].astype(BF16)
-        msg_ref[p, 16:, :] = vec_ref[p * share : (p + 1) * share, :].astype(BF16)
-    for f in range(2):
-        ghost_ref[f] = tot_ref[(halves + f) * 16 : (halves + f + 1) * 16, :].astype(BF16)
-
-
-def message_copies(msg_ref, ghost_ref, msg_in, ghost_in, msg_sems, ghost_sems):
-    brick, part, _, parts = here()
-    copies = []
-    for j in range(1, parts):
-        other = lax.rem(part + j, parts)
-        copies.append(
-            pltpu.make_async_remote_copy(
-                src_ref=msg_ref.at[other],
-                dst_ref=msg_in.at[j],
-                send_sem=msg_sems.at[0, j],
-                recv_sem=msg_sems.at[1, j],
-                device_id=(brick, other),
-                device_id_type=MESH,
-            )
-        )
-    for j in range(parts):
-        other = lax.rem(part + j, parts)
-        for f, side in enumerate(sides()):
-            copies.append(
-                pltpu.make_async_remote_copy(
-                    src_ref=ghost_ref.at[f],
-                    dst_ref=ghost_in.at[f, j],
-                    send_sem=ghost_sems.at[0, f, j],
-                    recv_sem=ghost_sems.at[1, f, j],
-                    device_id=(side, other),
-                    device_id_type=MESH,
-                )
-            )
-    return copies
-
-
-def finish(msg_ref, msg_in, ghost_in, send_refs, out_ref):
-    brick, part, bricks, parts = here()
-    share = msg_ref.shape[1] - 16
-    total = msg_ref[part].astype(F32)
-    for j in range(1, parts):
-        total = total + msg_in[j].astype(F32)
-    mine, vec = total[:16], total[16:]
-    half = part * share // LANES
-    slot = half * LANES + lax.broadcasted_iota(jnp.int32, (LANES, LANES), 0)
-    exists = (brick < bricks - 1, brick > 0)
-    for f in range(2):
-        ghosts = ghost_in[f, 0].astype(F32)
-        for j in range(1, parts):
-            ghosts = ghosts + ghost_in[f, j].astype(F32)
-        ghosts = jnp.where(exists[f], ghosts, 0.0)
-        hits = jnp.where(slot == send_refs[1 - f][...], 1.0, 0.0)
-        high = ghosts.astype(BF16)
-        low = (ghosts - high.astype(F32)).astype(BF16)
-        both = lax.dot_general(
-            jnp.concatenate([high, low], axis=0), hits.astype(BF16), NT, preferred_element_type=F32
-        )
-        row = lax.broadcasted_iota(jnp.int32, (16, LANES), 0)
-        mine = mine + jnp.where(row < 9, both[:16] + both[16:], 0.0)
-    shift = lax.rem(LANES - lax.rem(part * share, LANES), LANES)
-    mine = pltpu.roll(mine, shift, 1)
-    squares = lax.dot_general(
-        jnp.ones((16, vec.shape[1]), F32), vec * vec, NT, precision=lax.Precision.HIGHEST, preferred_element_type=F32
-    )
-    out_ref[...] = mine
-    out_ref[10:11, :share] = squares[10:11]
-
-VM = pl.BlockSpec(memory_space=pltpu.VMEM)
-HBM = pl.BlockSpec(memory_space=pl.ANY)
+def halo_place(rim_ref, table_ref, own, odd):
+    mate, cross = rim_ref[0], rim_ref[1]
+    table_ref[:, own : own + LANES] = jnp.where(odd == 1, mate, cross)
+    table_ref[:, own + LANES : own + 2 * LANES] = jnp.where(odd == 1, cross, mate)
+
+
+def deliver(ghosts, slots):
+    high = ghosts.astype(BF16)
+    low = (ghosts - high.astype(F32)).astype(BF16)
+    both = lax.dot_general(jnp.concatenate([high, low], axis=0), slots, NT, preferred_element_type=F32)
+    row = lax.broadcasted_iota(jnp.int32, (16, both.shape[1]), 0)
+    return jnp.where(row < 9, both[:16] + both[16:], 0.0)
+
+
+def slots_of(send, first, count):
+    slot = first + lax.broadcasted_iota(jnp.int32, (count, LANES), 0)
+    return jnp.where(slot == send, 1.0, 0.0).astype(BF16)
 
 
 def brick(pos, species, live, nb, mask, send_lo, send_hi, sparse, alpha, factor, parts):
     own, count = pos.shape[1], nb.shape[0]
     depth, rank = sparse.shape[1], factor.shape[1]
-    tables = own // LANES + 2
+    halves = own // LANES
+    tables = halves + 2
     share = own // parts
     names = scratch_shapes(own, count, tables * LANES, sparse.shape[0], depth, rank)
+    inputs = (pos, species, send_lo, send_hi, nb, mask, alpha, sparse, factor)
     names.update(
         table=pltpu.VMEM((8, tables * LANES), F32),
         face=pltpu.VMEM((2, 8, LANES), F32),
         rim=pltpu.VMEM((2, 8, LANES), F32),
-        sparse=pltpu.VMEM(sparse.shape, BF16),
-        factor=pltpu.VMEM(factor.shape, BF16),
         vec=pltpu.VMEM((own, rank), F32),
         tot=pltpu.VMEM((tables * 16, LANES), F32),
-        msg=pltpu.VMEM((parts, 16 + share, rank), BF16),
-        msg_in=pltpu.VMEM((parts, 16 + share, rank), BF16),
-        ghost=pltpu.VMEM((2, 16, LANES), BF16),
-        ghost_in=pltpu.VMEM((2, parts, 16, LANES), BF16),
-        halo_send=pltpu.SemaphoreType.DMA((2,)),
-        halo_recv=pltpu.SemaphoreType.DMA((2,)),
-        msg_sems=pltpu.SemaphoreType.DMA((2, parts)),
-        ghost_sems=pltpu.SemaphoreType.DMA((2, 2, parts)),
-        load_sems=pltpu.SemaphoreType.DMA((2,)),
+        vec_out=pltpu.VMEM((own, rank), BF16),
+        vec_in=pltpu.VMEM((parts, share, rank), BF16),
+        tot_out=pltpu.VMEM((halves, 16, LANES), BF16),
+        tot_in=pltpu.VMEM((parts, 16, LANES), BF16),
+        relay_out=pltpu.VMEM((16, LANES), F32),
+        relay_in=pltpu.VMEM((16, LANES), F32),
+        cross_out=pltpu.VMEM((16, LANES), BF16),
+        cross_in=pltpu.VMEM((parts, 16, LANES), BF16),
+        halo_sems=pltpu.SemaphoreType.DMA((2, 2)),
+        relay_sems=pltpu.SemaphoreType.DMA((2, 1)),
+        vec_sems=pltpu.SemaphoreType.DMA((2, parts)),
+        tot_sems=pltpu.SemaphoreType.DMA((2, parts)),
+        cross_sems=pltpu.SemaphoreType.DMA((2, parts)),
+        load_sems=pltpu.SemaphoreType.DMA((len(inputs) + 1,)),
+        live=pltpu.SMEM((1,), jnp.int32),
     )
     keys = list(names)
-
-    def kernel(
-        live_ref, pos_ref, species_ref, nb_ref, mask_ref, lo_ref, hi_ref, alpha_ref, sparse_hbm, factor_hbm, out_ref, *scratch
-    ):
-        s = dict(zip(keys, scratch))
-        peers = all_peers()
-        barrier = pltpu.get_barrier_semaphore()
-        for peer in peers:
-            pl.semaphore_signal(barrier, inc=1, device_id=peer, device_id_type=MESH)
+    local = [pltpu.VMEM(x.shape, x.dtype) for x in inputs]
+
+    def kernel(*refs):
+        sources, live_hbm, out_ref = refs[: len(inputs)], refs[len(inputs)], refs[len(inputs) + 1]
+        held = refs[len(inputs) + 2 : 2 * len(inputs) + 2]
+        s = dict(zip(keys, refs[2 * len(inputs) + 2 :]))
+        pos_ref, species_ref, lo_ref, hi_ref, nb_ref, mask_ref, alpha_ref, sparse_ref, factor_ref = held
+        place = Place()
+        place.greet()
         loads = [
-            pltpu.make_async_copy(sparse_hbm, s["sparse"], s["load_sems"].at[0]),
-            pltpu.make_async_copy(factor_hbm, s["factor"], s["load_sems"].at[1]),
+            pltpu.make_async_copy(x, y, s["load_sems"].at[k])
+            for k, (x, y) in enumerate(zip((*sources, live_hbm), (*held, s["live"])))
         ]
         for load in loads:
             load.start()
+        for load in loads[:4]:
+            load.wait()
         halo_pick(pos_ref, species_ref, (lo_ref, hi_ref), s["table"], s["face"])
+        place.met()
+        near = remote(s["face"].at[1 - place.odd], s["rim"].at[0], s["halo_sems"], (0,), (place.mate, place.part))
+        far = remote(s["face"].at[place.odd], s["rim"].at[1], s["halo_sems"], (1,), (place.cross, place.part))
+        near.start()
+
+        @pl.when(place.exists)
+        def _():
+            far.start()
+
+        @pl.when(jnp.logical_not(place.exists))
+        def _():
+            s["rim"][1] = jnp.zeros((8, LANES), F32)
+            for j in range(parts):
+                s["cross_in"][j] = jnp.zeros((16, LANES), BF16)
+
         identities(s["eye"])
-        for load in loads:
+        for load in loads[4:]:
             load.wait()
-        norms(s["sparse"], alpha_ref, s["scale"], 0, 2)
-        pl.semaphore_wait(barrier, len(peers))
-        halos = halo_copies(s["face"], s["rim"], s["halo_send"], s["halo_recv"])
-        for copy in halos:
-            copy.start()
-        norms(s["sparse"], alpha_ref, s["scale"], 2, sparse.shape[0] // 512)
-        for copy in halos:
-            copy.wait()
-        halo_place(s["rim"], s["table"], own)
-        pair_setup(s["table"], pos_ref, nb_ref, mask_ref, live_ref[0], s["off"], s["w"], s["sp"], s["r"])
+        norms(sparse_ref, alpha_ref, s["scale"], 0, sparse.shape[0] // 512)
+        near.wait()
+
+        @pl.when(place.exists)
+        def _():
+            far.wait()
+
+        halo_place(s["rim"], s["table"], own, place.odd)
+        pair_setup(s["table"], pos_ref, nb_ref, mask_ref, s["live"][0], s["off"], s["w"], s["sp"], s["r"])
         moments(s["off"], s["w"], s["r"], s["acc"], s["m"], s["mc"])
         descriptors(s["m"], s["mc"], s["d"], s["rinv"], s["desc"], s["eye"])
-        kernel_sums(s["desc"], s["sparse"], s["scale"], s["factor"], s["grad"], s["vec"], s["energy"])
+        kernel_sums(s["desc"], sparse_ref, s["scale"], factor_ref, s["grad"], s["vec"], s["energy"])
+        s["vec_out"][...] = s["vec"][...].astype(BF16)
+        vectors = [
+            remote(
+                s["vec_out"].at[pl.ds(pl.multiple_of(other * share, share), share)],
+                s["vec_in"].at[j],
+                s["vec_sems"],
+                (j,),
+                (place.brick, other),
+            )
+            for j, other in enumerate(place.others)
+            if j
+        ]
+        for copy in vectors:
+            copy.start()
         moment_grads(s["grad"], s["desc"], s["eye"], s["gd"], s["gt"], s["mc"], s["rinv"], s["g"])
         pair_terms(s["off"], s["sp"], s["r"], s["g"], s["t"], s["own"])
         scatter(nb_ref, s["t"], s["own"], s["energy"], s["tot"])
-        pack_messages(s["tot"], s["vec"], s["msg"], s["ghost"])
-        copies = message_copies(s["msg"], s["ghost"], s["msg_in"], s["ghost_in"], s["msg_sems"], s["ghost_sems"])
-        for copy in copies:
+        s["relay_out"][...] = s["tot"][pl.ds(pl.multiple_of((halves + 1 - place.odd) * 16, 16), 16), :]
+        relay = remote(s["relay_out"], s["relay_in"], s["relay_sems"], (0,), (place.mate, place.part))
+        relay.start()
+        s["cross_out"][...] = s["tot"][pl.ds(pl.multiple_of((halves + place.odd) * 16, 16), 16), :].astype(BF16)
+        crossing = [
+            remote(s["cross_out"], s["cross_in"].at[j], s["cross_sems"], (j,), (place.cross, other))
+            for j, other in enumerate(place.others)
+        ]
+
+        @pl.when(place.exists)
+        def _():
+            for copy in crossing[::-1]:
+                copy.start()
+
+        odd = place.odd == 1
+        near_send = jnp.where(odd, lo_ref[...], hi_ref[...])
+        far_send = jnp.where(odd, hi_ref[...], lo_ref[...])
+        near_slots = slots_of(near_send, 0, own)
+        relay.wait()
+        near_part = deliver(s["relay_in"][...], near_slots)
+        for h in range(halves):
+            s["tot_out"][h] = (
+                s["tot"][h * 16 : (h + 1) * 16, :] + near_part[:, h * LANES : (h + 1) * LANES]
+            ).astype(BF16)
+        totals = [
+            remote(
+                s["tot_out"].at[other * share // LANES], s["tot_in"].at[j], s["tot_sems"], (j,), (place.brick, other)
+            )
+            for j, other in enumerate(place.others)
+            if j
+        ]
+        for copy in totals:
             copy.start()
-        for copy in copies:
+        vec = s["vec_out"][pl.ds(pl.multiple_of(place.part * share, share), share), :].astype(F32)
+        for copy in vectors:
             copy.wait()
-        finish(s["msg"], s["msg_in"], s["ghost_in"], (lo_ref, hi_ref), out_ref)
-
+        for j in range(1, parts):
+            vec = vec + s["vec_in"][j].astype(F32)
+        variances = lax.dot_general(
+            jnp.ones((16, rank), F32), vec * vec, NT, precision=lax.Precision.HIGHEST, preferred_element_type=F32
+        )
+        half = place.part * share // LANES
+        far_slots = slots_of(far_send, half * LANES, LANES)
+        mine = s["tot_out"][half].astype(F32)
+        for copy in totals:
+            copy.wait()
+        for j in range(1, parts):
+            mine = mine + s["tot_in"][j].astype(F32)
+
+        @pl.when(place.exists)
+        def _():
+            for copy in crossing:
+                copy.wait()
+
+        ghosts = s["cross_in"][0].astype(F32)
+        for j in range(1, parts):
+            ghosts = ghosts + s["cross_in"][j].astype(F32)
+        mine = mine + deliver(ghosts, far_slots)
+        shift = lax.rem(LANES - lax.rem(place.part * share, LANES), LANES)
+        out_ref[...] = pltpu.roll(mine, shift, 1)
+        out_ref[10:11, :share] = variances[10:11]
+
+    anywhere = pl.BlockSpec(memory_space=pltpu.HBM)
     return pl.pallas_call(
         kernel,
         out_shape=jax.ShapeDtypeStruct((16, LANES), F32),
-        in_specs=[pl.BlockSpec(memory_space=pltpu.SMEM)] + [VM] * 7 + [HBM] * 2,
-        out_specs=VM,
-        scratch_shapes=list(names.values()),
+        in_specs=[anywhere] * (len(inputs) + 1),
+        out_specs=pl.BlockSpec(memory_space=pltpu.VMEM),
+        scratch_shapes=local + list(names.values()),
         compiler_params=pltpu.CompilerParams(
             vmem_limit_bytes=60 * 1024 * 1024, collective_id=0, has_side_effects=True
         ),
         name="brick",
-    )(live, pos, species, nb, mask, send_lo, send_hi, alpha, sparse, factor)
+    )(*inputs, live)
 
 
 def split(result, share):
@@ -545,11 +585,12 @@
         energy_ref[...] = result_ref[9:10, :share]
         variance_ref[...] = result_ref[10:11, :share]
 
+    vmem = pl.BlockSpec(memory_space=pltpu.VMEM)
     return pl.pallas_call(
         kernel,
         out_shape=tuple(jax.ShapeDtypeStruct((n, share), F32) for n in (3, 1, 1, 6)),
-        in_specs=[VM],
-        out_specs=(VM,) * 4,
+        in_specs=[vmem],
+        out_specs=(vmem,) * 4,
         name="split",
     )(result)
 

time: 39.7 us -> 32.4 us (0.82)
  the two profiles are of different devices: /device:TPU:32 before, /device:TPU:6 now
where the time goes in v2:
time: 32.4 us; the launch traced here: 32.3 us
  Pallas kernels  31 us (96%)
  between operations  1.29 us (4%)
    pallas_call x1, Pallas kernels, brick(): pl.pallas_call(kernel, out_shape=jax.ShapeDtypeStruct((16, LANES), F32),...  29.7 us
    pallas_call x1, Pallas kernels, split(): pl.pallas_call(kernel, out_shape=tuple((jax.ShapeDtypeStruct((n, share),...  1.3 us

profile of v2, /device:TPU:6, one launch (start us, length us, event | category | flops | bytes accessed | tf_op | source)
XLA Modules:
  0.0 32.3 jit_solution(3205562201269152146)
XLA Ops:
  1.3 29.7 %brick.1.result_ref = f32[16,128]{1,0:T(8,128)} custom-call(f32[3,256]{1,0:T(4,128)} %refs_0_.1, s32[1,256]{1,0:T(1,128)} %bitcast.7, s32[1,128]{1,0:T(1,128)} %bitcast.8, s32[1,128]{1,0:T(1,128)} %bitcast.9, s32[64,256]{1,0:T(8,128)} %refs_4_.1, s32[64,256]{1,0:T(8,128)} %refs_5_.1, f32[20,128]{1,0:T(8,128)} %bitcast.6, bf16[2560,768]{1,0:T(8,128)(2,1)} %refs_7_.1, ...), custom_call_target="tpu_custom_call" | custom-call | tf_op jit(solution)/shard_map/brick/pallas_call | solution.py:568
  30.9 1.3 %split.1 = (f32[3,32]{1,0:T(4,128)}, f32[1,32]{1,0:T(1,128)}, f32[1,32]{1,0:T(1,128)}, f32[6,32]{1,0:T(8,128)}) custom-call(f32[16,128]{1,0:T(8,128)} %brick.1.result_ref), custom_call_target="tpu_custom_call" | custom-call | tf_op jit(solution)/shard_map/split/pallas_call | solution.py:589

commit v3 on v2

--- a/solution.py
+++ b/solution.py
@@ -10,6 +10,7 @@
 SPECIES, RADIAL = 4, 4
 K = SPECIES * RADIAL
 LANES = 128
+LOW = 64
 RATES = tuple(scale * 2.0**r for scale in (0.1, 0.15) for r in range(RADIAL))
 ORDERS = ((0, 1), (1, 4), (4, 10))
 FOLD = (1.0,) * 7 + (2.0,) * 3
@@ -43,8 +44,37 @@
         scale_ref[:, t * chunk : (t + 1) * chunk] = inverse * jnp.where(row == 0, 1.0, 2.0 * alpha)
 
 
-def pair_setup(table_ref, pos_ref, nb_ref, mask_ref, live, off_ref, w_ref, sp_ref, r_ref):
+def pick_from(table_ref, first, last, low, high, value, rows):
+    picked = []
+    for c in range(4):
+        got = value[c]
+        for t in range(first, last):
+            source = jnp.broadcast_to(table_ref[c : c + 1, t * LANES : (t + 1) * LANES], (rows, LANES))
+            part = jnp.take_along_axis(source, low, axis=1, mode="promise_in_bounds")
+            got = part if got is None else jnp.where(high == t, part, got)
+        picked.append(got)
+    return picked
+
+
+def own_setup(table_ref, nb_ref, pick_ref):
+    halves, _, count, _ = pick_ref.shape
+    blocks = count // 8
+
+    def step(i, _):
+        h, b = i // blocks, i % blocks
+        rows = along(b * 8, 8)
+        index = nb_ref[rows, along(h * LANES, LANES)]
+        values = pick_from(table_ref, 0, halves, index & (LANES - 1), index // LANES, [None] * 4, 8)
+        for c in range(4):
+            pick_ref[h, c, rows, :] = values[c]
+        return 0
+
+    lax.fori_loop(0, halves * blocks, step, 0, unroll=8)
+
+
+def pair_setup(table_ref, pos_ref, nb_ref, mask_ref, live, pick_ref, off_ref, w_ref, kind_ref, r_ref):
     own = pos_ref.shape[1]
+    halves = own // LANES
     tables = table_ref.shape[1] // LANES
     blocks = nb_ref.shape[0] // 8
     lane = lax.broadcasted_iota(jnp.int32, (8, LANES), 1)
@@ -53,34 +83,26 @@
         h, b = i // blocks, i % blocks
         rows, cols = along(b * 8, 8), along(h * LANES, LANES)
         index = nb_ref[rows, cols]
-        low, high = index & (LANES - 1), index // LANES
-        picked = []
-        for c in range(4):
-            value = None
-            for t in range(tables):
-                source = jnp.broadcast_to(table_ref[c : c + 1, t * LANES : (t + 1) * LANES], (8, LANES))
-                part = jnp.take_along_axis(source, low, axis=1, mode="promise_in_bounds")
-                value = part if value is None else jnp.where(high == t, part, value)
-            picked.append(value)
+        held = [pick_ref[h, c, rows, :] for c in range(4)]
+        picked = pick_from(table_ref, halves, tables, index & (LANES - 1), index // LANES, held, 8)
         o = [picked[p] - pos_ref[p : p + 1, cols] for p in range(3)]
         alive = ((index >= own) | (index < live)) & (h * LANES + lane < live)
         valid = jnp.where(alive, mask_ref[rows, cols].astype(F32), 0.0)
         for p in range(3):
             off_ref[h, p, rows, :] = o[p]
-        for s in range(SPECIES):
-            w_ref[h, s, rows, :] = jnp.where(picked[3] == s, valid, 0.0)
-        sp_ref[h, 0, rows, :] = picked[3]
-        sp_ref[h, 1, rows, :] = valid
+        for s in range(SPECIES - 1):
+            w_ref[h, s, rows, :] = jnp.where(picked[3] == s, 1.0, 0.0)
+        kind_ref[h, rows, :] = picked[3].astype(jnp.int32)
         square = o[0] * o[0] + o[1] * o[1] + o[2] * o[2]
         for e in range(2):
             radial = jnp.exp(square * (-RATES[e * RADIAL]))
             for r in range(RADIAL):
                 if r:
                     radial = radial * radial
-                r_ref[h, e * RADIAL + r, rows, :] = radial
+                r_ref[h, e * RADIAL + r, rows, :] = radial * valid
         return 0
 
-    lax.fori_loop(0, own // LANES * blocks, step, 0, unroll=8)
+    lax.fori_loop(0, halves * blocks, step, 0, unroll=8)
 
 
 def moments(off_ref, w_ref, r_ref, acc_ref, m_ref, mc_ref):
@@ -94,13 +116,14 @@
             rows = slice(b * 8, b * 8 + 8)
             v = angular(r_ref[h, er, rows, :], [off_ref[h, p, rows, :] for p in range(3)])
             for s in range(SPECIES):
-                weight = w_ref[h, s, rows, :]
+                weight = w_ref[h, s, rows, :] if s < SPECIES - 1 else None
                 for m in range(10):
-                    term = weight * v[m]
+                    term = v[m] if weight is None else weight * v[m]
                     total[s][m] = term if b == 0 else total[s][m] + term
         e, r = er // RADIAL, er % RADIAL
-        for s in range(SPECIES):
-            for m in range(10):
+        for m in range(10):
+            total[3][m] = total[3][m] - (total[0][m] + total[1][m] + total[2][m])
+            for s in range(SPECIES):
                 acc_ref[(h * 2 + e) * 10 + m, along((s * RADIAL + r) * 8, 8), :] = total[s][m]
         return 0
 
@@ -117,52 +140,46 @@
     lax.fori_loop(0, halves * 20, fold, 0, unroll=8)
 
 
-def descriptors(m_ref, mc_ref, d_ref, rinv_ref, desc_ref, eye_ref):
+def descriptors(m_ref, mc_ref, d_ref, rinv_ref, desc_ref, plain_ref):
     halves = d_ref.shape[0]
-    for h in range(halves):
-        base = h * 20
-
-        def step(k, squares):
+
+    def step(k, squares):
+        fresh = []
+        for h in range(halves):
+            base = h * 20
+            total = squares[h]
             for l, (start, stop) in enumerate(ORDERS):
                 value = None
                 for m in range(start, stop):
                     term = m_ref[base + m, pl.ds(k, 1), :] * mc_ref[base + 10 + m]
                     value = term if value is None else value + term
                 d_ref[h, along(l * K * K + k * K, K), :] = value
-                squares = squares + value * value
-            return squares
-
-        squares = lax.fori_loop(0, K, step, jnp.zeros((K, LANES), F32), unroll=2)
-        rinv = lax.rsqrt(jnp.sum(squares, axis=0, keepdims=True) + EPS)
+                total = total + value * value
+            fresh.append(total)
+        return tuple(fresh)
+
+    squares = lax.fori_loop(0, K, step, (jnp.zeros((K, LANES), F32),) * halves, unroll=8)
+    for h in range(halves):
+        rinv = lax.rsqrt(jnp.sum(squares[h], axis=0, keepdims=True) + EPS)
         rinv_ref[h] = jnp.broadcast_to(rinv, (8, LANES))
         unit = (d_ref[h] * rinv).astype(BF16)
         desc_ref[h * LANES : (h + 1) * LANES, :] = lax.dot_general(
-            eye_ref[:LANES, :LANES], unit, NT, preferred_element_type=F32
+            plain_ref[...], unit, NT, preferred_element_type=F32
         ).astype(BF16)
 
 
-def kernel_sums(desc_ref, sparse_ref, scale_ref, factor_ref, grad_ref, vec_ref, energy_ref, chunk=512):
-    count = sparse_ref.shape[0]
-    for t in range(count // chunk):
-        rows = slice(t * chunk, (t + 1) * chunk)
-        raw = sparse_ref[rows, :]
-        projection = lax.dot_general(desc_ref[...], raw, NT, preferred_element_type=F32)
-        coefficient = projection * scale_ref[1:2, rows]
-        kernel = projection * projection * scale_ref[0:1, rows]
-        energy_terms = coefficient * projection
-        energy = energy_terms[:, :LANES]
-        for j in range(1, chunk // LANES):
-            energy = energy + energy_terms[:, j * LANES : (j + 1) * LANES]
-        grad = jnp.dot(coefficient.astype(BF16), raw, preferred_element_type=F32)
-        vec = jnp.dot(kernel.astype(BF16), factor_ref[rows, :], preferred_element_type=F32)
-        if t == 0:
-            grad_ref[...] = grad
-            vec_ref[...] = vec
-            energy_ref[...] = energy
-        else:
-            grad_ref[...] += grad
-            vec_ref[...] += vec
-            energy_ref[...] += energy
+def kernel_sums(desc_ref, sparse_ref, scale_ref, factor_ref, grad_ref, vec_ref, energy_ref):
+    raw = sparse_ref[...]
+    projection = lax.dot_general(desc_ref[...], raw, NT, preferred_element_type=F32)
+    coefficient = projection * scale_ref[1:2, :]
+    kernel = projection * projection * scale_ref[0:1, :]
+    energy_terms = coefficient * projection
+    energy = energy_terms[:, :LANES]
+    for j in range(1, raw.shape[0] // LANES):
+        energy = energy + energy_terms[:, j * LANES : (j + 1) * LANES]
+    energy_ref[...] = energy
+    grad_ref[...] = jnp.dot(coefficient.astype(BF16), raw, preferred_element_type=F32)
+    vec_ref[...] = jnp.dot(kernel.astype(BF16), factor_ref[...], preferred_element_type=F32)
 
 
 def moment_grads(grad_ref, desc_ref, eye_ref, gd_ref, gt_ref, mc_ref, rinv_ref, g_ref):
@@ -197,20 +214,18 @@
     lax.fori_loop(0, halves * 2, step, 0)
 
 
-def pair_terms(off_ref, sp_ref, r_ref, g_ref, t_ref, own_ref, group=2):
+def pair_terms(off_ref, kind_ref, r_ref, g_ref, t_ref, own_ref, group=2):
     halves, _, count, _ = off_ref.shape
     blocks = count // 8 // group
     own_ref[...] = jnp.zeros(own_ref.shape, F32)
-    for h in range(halves):
-        t_ref[h, 9 * count :, :] = jnp.zeros((7 * count, LANES), F32)
 
     def step(i, _):
         h, b = i // blocks, i % blocks
         rows = [along((b * group + q) * 8, 8) for q in range(group)]
         o = [[off_ref[h, p, rows[q], :] for p in range(3)] for q in range(group)]
         ang = [[None] + o[q] + [o[q][x] * o[q][y] for x, y in PAIRS] for q in range(group)]
-        kind = [sp_ref[h, 0, rows[q], :] for q in range(group)]
-        hit = [[kind[q] == s for s in range(3)] for q in range(group)]
+        kind = [kind_ref[h, rows[q], :] for q in range(group)]
+        which = [[kind[q], kind[q] + SPECIES] for q in range(group)]
         top = [[None] * 10 for _ in range(group)]
         slope = [None] * group
         for er, rate in enumerate(RATES):
@@ -218,9 +233,9 @@
             radial = [r_ref[h, er, rows[q], :] for q in range(group)]
             inner = [None] * group
             for m in range(10):
-                g = [g_ref[(h * 2 + e) * 10 + m, s * RADIAL + r : s * RADIAL + r + 1, :] for s in range(SPECIES)]
+                g = g_ref[(h * 2 + e) * 10 + m, r // 2 * 8 : r // 2 * 8 + 8, :]
                 for q in range(group):
-                    pick = jnp.where(hit[q][0], g[0], jnp.where(hit[q][1], g[1], jnp.where(hit[q][2], g[2], g[3])))
+                    pick = jnp.take_along_axis(g, which[q][r % 2], axis=0, mode="promise_in_bounds")
                     if m == 0:
                         inner[q] = pick
                     else:
@@ -234,10 +249,9 @@
         for q in range(group):
             x, y, z = o[q]
             t = top[q]
-            valid = sp_ref[h, 1, rows[q], :]
-            gx = valid * (t[1] + 2.0 * x * (t[4] + slope[q]) + t[7] * y + t[8] * z)
-            gy = valid * (t[2] + 2.0 * y * (t[5] + slope[q]) + t[7] * x + t[9] * z)
-            gz = valid * (t[3] + 2.0 * z * (t[6] + slope[q]) + t[8] * x + t[9] * y)
+            gx = t[1] + 2.0 * x * (t[4] + slope[q]) + t[7] * y + t[8] * z
+            gy = t[2] + 2.0 * y * (t[5] + slope[q]) + t[7] * x + t[9] * z
+            gz = t[3] + 2.0 * z * (t[6] + slope[q]) + t[8] * x + t[9] * y
             g = [gx, gy, gz]
             terms = [-v for v in g] + [-0.5 * o[q][a] * g[c] for a, c in PAIRS]
             for c in range(9):
@@ -250,62 +264,84 @@
     lax.fori_loop(0, halves * blocks, step, 0)
 
 
-def scatter(nb_ref, t_ref, own_ref, energy_ref, tot_ref, unroll=32):
+def scatter(nb_ref, t_ref, own_ref, energy_ref, tot_ref, unroll=16):
     count, own = nb_ref.shape
     halves = own // LANES
     tables = tot_ref.shape[0] // 16
-    slot = lax.broadcasted_iota(jnp.int32, (LANES, own), 0).astype(F32).astype(BF16)
+    groups = tables * LANES // LOW
+    per = LANES // LOW
+    slot = lax.broadcasted_iota(jnp.int32, (LOW, own), 0).astype(F32).astype(BF16)
+    row = lax.broadcasted_iota(jnp.int32, (16, own), 0)
+    upper = jnp.where(row < 8, 0, 1).astype(F32).astype(BF16)
+    every = row.astype(F32).astype(BF16)
 
     def step(i, total):
         left, right = [], []
         for u in range(unroll):
             n = i * unroll + u
             index = jnp.broadcast_to(nb_ref[pl.ds(n, 1), :], (16, own))
-            low = (index & (LANES - 1)).astype(F32).astype(BF16)
-            high = (index // LANES).astype(F32).astype(BF16)
-            terms = jnp.concatenate(
-                [t_ref[h, pl.ds(n, 16, stride=count), :] for h in range(halves)], axis=1
-            ).astype(BF16)
-            zero, one = jnp.zeros_like(terms), jnp.ones_like(terms)
-            left.append(jnp.concatenate([jnp.where(high == t, terms, zero) for t in range(tables)], axis=0))
+            low = (index & (LOW - 1)).astype(F32).astype(BF16)
+            high = (index // LOW).astype(F32).astype(BF16)
+            eight = jnp.concatenate([t_ref[h, pl.ds(n, 8, stride=count), :] for h in range(halves)], axis=1)
+            eight = jnp.concatenate([eight, eight], axis=0).astype(BF16)
+            ninth = jnp.concatenate([t_ref[h, pl.ds(8 * count + n, 1), :] for h in range(halves)], axis=1)
+            ninth = jnp.broadcast_to(ninth, (16, own)).astype(BF16)
+            zero, one = jnp.zeros_like(eight), jnp.ones_like(eight)
+            shifted = high - upper
+            left.append(
+                jnp.concatenate(
+                    [jnp.where(shifted == g, eight, zero) for g in range(0, groups, 2)]
+                    + [jnp.where(high == every, ninth, zero)],
+                    axis=0,
+                )
+            )
             right.append(
-                jnp.concatenate(
-                    [jnp.where(slot[j : j + 16] == low, one, zero) for j in range(0, LANES, 16)], axis=0
-                )
+                jnp.concatenate([jnp.where(slot[j : j + 16] == low, one, zero) for j in range(0, LOW, 16)], axis=0)
             )
         return total + lax.dot_general(
             jnp.concatenate(left, axis=1), jnp.concatenate(right, axis=1), NT, preferred_element_type=F32
         )
 
-    total = lax.fori_loop(0, count // unroll, step, jnp.zeros(tot_ref.shape, F32))
+    total = lax.fori_loop(0, count // unroll, step, jnp.zeros((groups * 8 + 16, LOW), F32))
     energies = 0.5 * lax.dot_general(
         jnp.ones((16, LANES), F32), energy_ref[...], NT, precision=lax.Precision.HIGHEST, preferred_element_type=F32
     )
-    row = lax.broadcasted_iota(jnp.int32, (16, LANES), 0)
-    for h in range(halves):
-        mine = own_ref[h, pl.ds(0, 16, stride=8), :]
-        for j in range(1, 8):
-            mine = mine + own_ref[h, pl.ds(j, 16, stride=8), :]
-        mine = jnp.where(row == 9, energies[:, h * LANES : (h + 1) * LANES], mine)
-        tot_ref[h * 16 : (h + 1) * 16, :] = total[h * 16 : (h + 1) * 16, :] + mine
-    for t in range(halves, tables):
-        tot_ref[t * 16 : (t + 1) * 16, :] = total[t * 16 : (t + 1) * 16, :]
-
-
-def identities(eye_ref):
+    row = lax.broadcasted_iota(jnp.int32, (8, LANES), 0)
+    for t in range(tables):
+        main = jnp.concatenate([total[(t * per + g) * 8 : (t * per + g + 1) * 8] for g in range(per)], axis=1)
+        last = jnp.concatenate(
+            [total[groups * 8 + t * per + g : groups * 8 + t * per + g + 1] for g in range(per)], axis=1
+        )
+        rest = jnp.where(row == 0, last, 0.0)
+        if t < halves:
+            mine = own_ref[t, pl.ds(0, 16, stride=8), :]
+            for j in range(1, 8):
+                mine = mine + own_ref[t, pl.ds(j, 16, stride=8), :]
+            main = main + mine[:8]
+            rest = rest + jnp.where(row == 1, energies[:8, t * LANES : (t + 1) * LANES], mine[8:])
+        tot_ref[t * 16 : t * 16 + 8, :] = main
+        tot_ref[t * 16 + 8 : t * 16 + 16, :] = rest
+
+
+def identities(plain_ref, eye_ref):
     size = K * K
     row = lax.broadcasted_iota(jnp.int32, (size, size), 0)
     col = lax.broadcasted_iota(jnp.int32, (size, size), 1)
-    eye_ref[:size, :] = jnp.where(row == col, 1.0, 0.0).astype(BF16)
-    eye_ref[size:, :] = jnp.where((row % K) * K + row // K == col, 1.0, 0.0).astype(BF16)
+    plain_ref[...] = jnp.where(row[:LANES, :LANES] == col[:LANES, :LANES], 1.0, 0.0).astype(BF16)
+    outer = row // K
+    inner = row % SPECIES * RADIAL + row % K // SPECIES
+    eye_ref[:size, :] = jnp.where(outer * K + inner == col, 1.0, 0.0).astype(BF16)
+    eye_ref[size:, :] = jnp.where(inner * K + outer == col, 1.0, 0.0).astype(BF16)
 
 
 def scratch_shapes(own, count, width, sparse, depth, rank):
     halves = own // LANES
     return dict(
         off=pltpu.VMEM((halves, 3, count, LANES), F32),
-        w=pltpu.VMEM((halves, SPECIES, count, LANES), F32),
-        sp=pltpu.VMEM((halves, 2, count, LANES), F32),
+        pick=pltpu.VMEM((halves, 4, count, LANES), F32),
+        plain=pltpu.VMEM((LANES, LANES), BF16),
+        w=pltpu.VMEM((halves, SPECIES - 1, count, LANES), F32),
+        kind=pltpu.VMEM((halves, count, LANES), jnp.int32),
         r=pltpu.VMEM((halves, len(RATES), count, LANES), F32),
         acc=pltpu.VMEM((halves * 20, K * 8, LANES), F32),
         m=pltpu.VMEM((halves * 20, K, LANES), F32),
@@ -320,7 +356,7 @@
         gd=pltpu.VMEM((own, depth), BF16),
         gt=pltpu.VMEM((halves, 3, 2 * K * K, LANES), F32),
         g=pltpu.VMEM((halves * 20, K, LANES), F32),
-        t=pltpu.VMEM((halves, 16 * count, LANES), F32),
+        t=pltpu.VMEM((halves, 9 * count, LANES), F32),
         own=pltpu.VMEM((halves, 16 * 8, LANES), F32),
     )
 
@@ -413,7 +449,7 @@
     tables = halves + 2
     share = own // parts
     names = scratch_shapes(own, count, tables * LANES, sparse.shape[0], depth, rank)
-    inputs = (pos, species, send_lo, send_hi, nb, mask, alpha, sparse, factor)
+    inputs = (pos, species, send_lo, send_hi, nb, mask, alpha, sparse, factor, live)
     names.update(
         table=pltpu.VMEM((8, tables * LANES), F32),
         face=pltpu.VMEM((2, 8, LANES), F32),
@@ -433,22 +469,21 @@
         vec_sems=pltpu.SemaphoreType.DMA((2, parts)),
         tot_sems=pltpu.SemaphoreType.DMA((2, parts)),
         cross_sems=pltpu.SemaphoreType.DMA((2, parts)),
-        load_sems=pltpu.SemaphoreType.DMA((len(inputs) + 1,)),
-        live=pltpu.SMEM((1,), jnp.int32),
+        load_sems=pltpu.SemaphoreType.DMA((len(inputs),)),
     )
     keys = list(names)
     local = [pltpu.VMEM(x.shape, x.dtype) for x in inputs]
 
     def kernel(*refs):
-        sources, live_hbm, out_ref = refs[: len(inputs)], refs[len(inputs)], refs[len(inputs) + 1]
-        held = refs[len(inputs) + 2 : 2 * len(inputs) + 2]
-        s = dict(zip(keys, refs[2 * len(inputs) + 2 :]))
-        pos_ref, species_ref, lo_ref, hi_ref, nb_ref, mask_ref, alpha_ref, sparse_ref, factor_ref = held
+        sources, out_ref = refs[: len(inputs)], refs[len(inputs)]
+        held = refs[len(inputs) + 1 : 2 * len(inputs) + 1]
+        s = dict(zip(keys, refs[2 * len(inputs) + 1 :]))
+        pos_ref, species_ref, lo_ref, hi_ref, nb_ref, mask_ref, alpha_ref, sparse_ref, factor_ref, live_ref = held
         place = Place()
         place.greet()
         loads = [
             pltpu.make_async_copy(x, y, s["load_sems"].at[k])
-            for k, (x, y) in enumerate(zip((*sources, live_hbm), (*held, s["live"])))
+            for k, (x, y) in enumerate(zip(sources, held))
         ]
         for load in loads:
             load.start()
@@ -470,10 +505,11 @@
             for j in range(parts):
                 s["cross_in"][j] = jnp.zeros((16, LANES), BF16)
 
-        identities(s["eye"])
+        identities(s["plain"], s["eye"])
         for load in loads[4:]:
             load.wait()
         norms(sparse_ref, alpha_ref, s["scale"], 0, sparse.shape[0] // 512)
+        own_setup(s["table"], nb_ref, s["pick"])
         near.wait()
 
         @pl.when(place.exists)
@@ -481,9 +517,12 @@
             far.wait()
 
         halo_place(s["rim"], s["table"], own, place.odd)
-        pair_setup(s["table"], pos_ref, nb_ref, mask_ref, s["live"][0], s["off"], s["w"], s["sp"], s["r"])
+        live_row = jnp.broadcast_to(live_ref[...], (8, LANES))
+        pair_setup(
+            s["table"], pos_ref, nb_ref, mask_ref, live_row, s["pick"], s["off"], s["w"], s["kind"], s["r"]
+        )
         moments(s["off"], s["w"], s["r"], s["acc"], s["m"], s["mc"])
-        descriptors(s["m"], s["mc"], s["d"], s["rinv"], s["desc"], s["eye"])
+        descriptors(s["m"], s["mc"], s["d"], s["rinv"], s["desc"], s["plain"])
         kernel_sums(s["desc"], sparse_ref, s["scale"], factor_ref, s["grad"], s["vec"], s["energy"])
         s["vec_out"][...] = s["vec"][...].astype(BF16)
         vectors = [
@@ -500,7 +539,7 @@
         for copy in vectors:
             copy.start()
         moment_grads(s["grad"], s["desc"], s["eye"], s["gd"], s["gt"], s["mc"], s["rinv"], s["g"])
-        pair_terms(s["off"], s["sp"], s["r"], s["g"], s["t"], s["own"])
+        pair_terms(s["off"], s["kind"], s["r"], s["g"], s["t"], s["own"])
         scatter(nb_ref, s["t"], s["own"], s["energy"], s["tot"])
         s["relay_out"][...] = s["tot"][pl.ds(pl.multiple_of((halves + 1 - place.odd) * 16, 16), 16), :]
         relay = remote(s["relay_out"], s["relay_in"], s["relay_sems"], (0,), (place.mate, place.part))
@@ -568,14 +607,14 @@
     return pl.pallas_call(
         kernel,
         out_shape=jax.ShapeDtypeStruct((16, LANES), F32),
-        in_specs=[anywhere] * (len(inputs) + 1),
+        in_specs=[anywhere] * len(inputs),
         out_specs=pl.BlockSpec(memory_space=pltpu.VMEM),
         scratch_shapes=local + list(names.values()),
         compiler_params=pltpu.CompilerParams(
             vmem_limit_bytes=60 * 1024 * 1024, collective_id=0, has_side_effects=True
         ),
         name="brick",
-    )(*inputs, live)
+    )(*inputs)
 
 
 def split(result, share):
@@ -602,7 +641,7 @@
     result = brick(
         positions,
         species[None],
-        live_count,
+        live_count[None],
         neighbors,
         neighbor_mask,
         send_lo[None],

time: 32.4 us -> 31 us (0.957)
  Pallas kernels: 31 us -> 29.5 us
    pallas_call x1, Pallas kernels: 29.7 us -> 28.2 us  [brick(): pl.pallas_call(kernel, out_shape=jax.ShapeDtypeStruct((16, LANES), F32),...]
where the time goes in v3:
time: 31 us; the launch traced here: 30.8 us
  Pallas kernels  29.5 us (95%)
  between operations  1.29 us (4%)
    pallas_call x1, Pallas kernels, brick(): pl.pallas_call(kernel, out_shape=jax.ShapeDtypeStruct((16, LANES), F32),...  28.2 us
    pallas_call x1, Pallas kernels, split(): pl.pallas_call(kernel, out_shape=tuple((jax.ShapeDtypeStruct((n, share),...  1.3 us

profile of v3, /device:TPU:6, one launch (start us, length us, event | category | flops | bytes accessed | tf_op | source)
XLA Modules:
  0.0 30.8 jit_solution(13432495492247409591)
XLA Ops:
  1.3 28.2 %brick.1.result_ref = f32[16,128]{1,0:T(8,128)} custom-call(f32[3,256]{1,0:T(4,128)} %refs_0_.1, s32[1,256]{1,0:T(1,128)} %bitcast.9, s32[1,128]{1,0:T(1,128)} %bitcast.10, s32[1,128]{1,0:T(1,128)} %bitcast.11, s32[64,256]{1,0:T(8,128)} %refs_4_.1, s32[64,256]{1,0:T(8,128)} %refs_5_.1, f32[20,128]{1,0:T(8,128)} %bitcast.8, bf16[2560,768]{1,0:T(8,128)(2,1)} %refs_7_.1, ...), custom_call_target="tpu_custom_call" | custom-call | tf_op jit(solution)/shard_map/brick/pallas_call | solution.py:607
  29.5 1.3 %split.1 = (f32[3,32]{1,0:T(4,128)}, f32[1,32]{1,0:T(1,128)}, f32[1,32]{1,0:T(1,128)}, f32[6,32]{1,0:T(8,128)}) custom-call(f32[16,128]{1,0:T(8,128)} %brick.1.result_ref), custom_call_target="tpu_custom_call" | custom-call | tf_op jit(solution)/shard_map/split/pallas_call | solution.py:628

commit v4 on v3

--- a/solution.py
+++ b/solution.py
@@ -107,37 +107,37 @@
 
 def moments(off_ref, w_ref, r_ref, acc_ref, m_ref, mc_ref):
     halves, _, count, _ = off_ref.shape
-    rates = len(RATES)
-
-    def step(i, _):
-        h, er = i // rates, i % rates
-        total = [[None] * 10 for _ in range(SPECIES)]
-        for b in range(count // 8):
-            rows = slice(b * 8, b * 8 + 8)
-            v = angular(r_ref[h, er, rows, :], [off_ref[h, p, rows, :] for p in range(3)])
-            for s in range(SPECIES):
-                weight = w_ref[h, s, rows, :] if s < SPECIES - 1 else None
-                for m in range(10):
-                    term = v[m] if weight is None else weight * v[m]
-                    total[s][m] = term if b == 0 else total[s][m] + term
-        e, r = er // RADIAL, er % RADIAL
-        for m in range(10):
-            total[3][m] = total[3][m] - (total[0][m] + total[1][m] + total[2][m])
-            for s in range(SPECIES):
-                acc_ref[(h * 2 + e) * 10 + m, along((s * RADIAL + r) * 8, 8), :] = total[s][m]
-        return 0
-
-    lax.fori_loop(0, halves * rates, step, 0)
-
-    def fold(i, _):
-        value = acc_ref[i, pl.ds(0, K, stride=8), :]
-        for j in range(1, 8):
-            value = value + acc_ref[i, pl.ds(j, K, stride=8), :]
-        m_ref[i] = value
-        mc_ref[i] = value * jnp.where(i % 10 >= 7, 2.0, 1.0)
-        return 0
-
-    lax.fori_loop(0, halves * 20, fold, 0, unroll=8)
+
+    def fold(i, ms):
+        for m in ms:
+            value = acc_ref[i * 10 + m, pl.ds(0, K, stride=8), :]
+            for j in range(1, 8):
+                value = value + acc_ref[i * 10 + m, pl.ds(j, K, stride=8), :]
+            m_ref[i * 10 + m] = value
+            mc_ref[i * 10 + m] = value * FOLD[m]
+
+    def step(i, before):
+        h, e = i // 2, i % 2
+        for r in range(RADIAL):
+            total = [[None] * 10 for _ in range(SPECIES)]
+            for b in range(count // 8):
+                rows = slice(b * 8, b * 8 + 8)
+                v = angular(r_ref[h, e * RADIAL + r, rows, :], [off_ref[h, p, rows, :] for p in range(3)])
+                for s in range(SPECIES):
+                    weight = w_ref[h, s, rows, :] if s < SPECIES - 1 else None
+                    for m in range(10):
+                        term = v[m] if weight is None else weight * v[m]
+                        total[s][m] = term if b == 0 else total[s][m] + term
+            if before is not None:
+                fold(before, range(r * 10 // RADIAL, (r + 1) * 10 // RADIAL))
+            for m in range(10):
+                total[3][m] = total[3][m] - (total[0][m] + total[1][m] + total[2][m])
+                for s in range(SPECIES):
+                    acc_ref[i * 10 + m, (s * RADIAL + r) * 8 : (s * RADIAL + r) * 8 + 8, :] = total[s][m]
+
+    for i in range(halves * 2):
+        step(i, i - 1 if i else None)
+    fold(halves * 2 - 1, range(10))
 
 
 def descriptors(m_ref, mc_ref, d_ref, rinv_ref, desc_ref, plain_ref):
@@ -188,14 +188,12 @@
     grad = grad_ref[...]
     along_unit = jnp.sum(grad * unit, axis=1, keepdims=True)
     gd_ref[...] = (grad - unit * along_unit).astype(BF16)
-    for h in range(halves):
-        for l in range(3):
-            gt_ref[h, l] = lax.dot_general(
-                eye_ref[...],
-                gd_ref[h * LANES : (h + 1) * LANES, l * K * K : (l + 1) * K * K],
-                NT,
-                preferred_element_type=F32,
-            )
+    for l in range(3):
+        turned = lax.dot_general(
+            eye_ref[...], gd_ref[:, l * K * K : (l + 1) * K * K], NT, preferred_element_type=F32
+        )
+        for h in range(halves):
+            gt_ref[h, l] = turned[:, h * LANES : (h + 1) * LANES]
 
     def step(i, _):
         h, e = i // 2, i % 2
@@ -264,40 +262,26 @@
     lax.fori_loop(0, halves * blocks, step, 0)
 
 
-def scatter(nb_ref, t_ref, own_ref, energy_ref, tot_ref, unroll=16):
+def scatter(nb_ref, hot_ref, t_ref, own_ref, energy_ref, tot_ref, unroll=32):
     count, own = nb_ref.shape
     halves = own // LANES
     tables = tot_ref.shape[0] // 16
     groups = tables * LANES // LOW
     per = LANES // LOW
-    slot = lax.broadcasted_iota(jnp.int32, (LOW, own), 0).astype(F32).astype(BF16)
-    row = lax.broadcasted_iota(jnp.int32, (16, own), 0)
-    upper = jnp.where(row < 8, 0, 1).astype(F32).astype(BF16)
-    every = row.astype(F32).astype(BF16)
+    row = lax.broadcasted_iota(jnp.int32, (8, own), 0)
 
     def step(i, total):
         left, right = [], []
         for u in range(unroll):
             n = i * unroll + u
-            index = jnp.broadcast_to(nb_ref[pl.ds(n, 1), :], (16, own))
-            low = (index & (LOW - 1)).astype(F32).astype(BF16)
-            high = (index // LOW).astype(F32).astype(BF16)
+            index = nb_ref[pl.ds(n, 1), :]
+            high = jnp.broadcast_to(index // LOW, (8, own))
             eight = jnp.concatenate([t_ref[h, pl.ds(n, 8, stride=count), :] for h in range(halves)], axis=1)
-            eight = jnp.concatenate([eight, eight], axis=0).astype(BF16)
             ninth = jnp.concatenate([t_ref[h, pl.ds(8 * count + n, 1), :] for h in range(halves)], axis=1)
-            ninth = jnp.broadcast_to(ninth, (16, own)).astype(BF16)
-            zero, one = jnp.zeros_like(eight), jnp.ones_like(eight)
-            shifted = high - upper
-            left.append(
-                jnp.concatenate(
-                    [jnp.where(shifted == g, eight, zero) for g in range(0, groups, 2)]
-                    + [jnp.where(high == every, ninth, zero)],
-                    axis=0,
-                )
-            )
-            right.append(
-                jnp.concatenate([jnp.where(slot[j : j + 16] == low, one, zero) for j in range(0, LOW, 16)], axis=0)
-            )
+            masked = [jnp.where(high == g, eight, 0.0) for g in range(groups)]
+            masked += [jnp.where(high == row, ninth, 0.0), jnp.zeros((8, own), F32)]
+            left.append(jnp.concatenate(masked, axis=0).astype(BF16))
+            right.append(hot_ref[n])
         return total + lax.dot_general(
             jnp.concatenate(left, axis=1), jnp.concatenate(right, axis=1), NT, preferred_element_type=F32
         )
@@ -321,6 +305,18 @@
             rest = rest + jnp.where(row == 1, energies[:8, t * LANES : (t + 1) * LANES], mine[8:])
         tot_ref[t * 16 : t * 16 + 8, :] = main
         tot_ref[t * 16 + 8 : t * 16 + 16, :] = rest
+
+
+def one_hots(nb_ref, hot_ref):
+    count, own = nb_ref.shape
+    slot = lax.broadcasted_iota(jnp.int32, (LOW, own), 0)
+
+    def step(n, _):
+        low = nb_ref[pl.ds(n, 1), :] & (LOW - 1)
+        hot_ref[n] = jnp.where(slot == low, 1.0, 0.0).astype(BF16)
+        return 0
+
+    lax.fori_loop(0, count, step, 0, unroll=4)
 
 
 def identities(plain_ref, eye_ref):
@@ -358,6 +354,7 @@
         g=pltpu.VMEM((halves * 20, K, LANES), F32),
         t=pltpu.VMEM((halves, 9 * count, LANES), F32),
         own=pltpu.VMEM((halves, 16 * 8, LANES), F32),
+        hot=pltpu.VMEM((count, LOW, own), BF16),
     )
 
 
@@ -442,14 +439,14 @@
     return jnp.where(slot == send, 1.0, 0.0).astype(BF16)
 
 
-def brick(pos, species, live, nb, mask, send_lo, send_hi, sparse, alpha, factor, parts):
+def brick(pos, species, nb, mask, send_lo, send_hi, sparse, alpha, factor, parts):
     own, count = pos.shape[1], nb.shape[0]
     depth, rank = sparse.shape[1], factor.shape[1]
     halves = own // LANES
     tables = halves + 2
     share = own // parts
     names = scratch_shapes(own, count, tables * LANES, sparse.shape[0], depth, rank)
-    inputs = (pos, species, send_lo, send_hi, nb, mask, alpha, sparse, factor, live)
+    inputs = (pos, species, send_lo, send_hi, nb, mask, alpha, sparse, factor)
     names.update(
         table=pltpu.VMEM((8, tables * LANES), F32),
         face=pltpu.VMEM((2, 8, LANES), F32),
@@ -478,7 +475,7 @@
         sources, out_ref = refs[: len(inputs)], refs[len(inputs)]
         held = refs[len(inputs) + 1 : 2 * len(inputs) + 1]
         s = dict(zip(keys, refs[2 * len(inputs) + 1 :]))
-        pos_ref, species_ref, lo_ref, hi_ref, nb_ref, mask_ref, alpha_ref, sparse_ref, factor_ref, live_ref = held
+        pos_ref, species_ref, lo_ref, hi_ref, nb_ref, mask_ref, alpha_ref, sparse_ref, factor_ref = held
         place = Place()
         place.greet()
         loads = [
@@ -510,6 +507,7 @@
             load.wait()
         norms(sparse_ref, alpha_ref, s["scale"], 0, sparse.shape[0] // 512)
         own_setup(s["table"], nb_ref, s["pick"])
+        one_hots(nb_ref, s["hot"])
         near.wait()
 
         @pl.when(place.exists)
@@ -517,7 +515,7 @@
             far.wait()
 
         halo_place(s["rim"], s["table"], own, place.odd)
-        live_row = jnp.broadcast_to(live_ref[...], (8, LANES))
+        live_row = jnp.broadcast_to(jnp.sum(mask_ref[0:1, :], axis=1, keepdims=True), (8, LANES))
         pair_setup(
             s["table"], pos_ref, nb_ref, mask_ref, live_row, s["pick"], s["off"], s["w"], s["kind"], s["r"]
         )
@@ -540,7 +538,7 @@
             copy.start()
         moment_grads(s["grad"], s["desc"], s["eye"], s["gd"], s["gt"], s["mc"], s["rinv"], s["g"])
         pair_terms(s["off"], s["kind"], s["r"], s["g"], s["t"], s["own"])
-        scatter(nb_ref, s["t"], s["own"], s["energy"], s["tot"])
+        scatter(nb_ref, s["hot"], s["t"], s["own"], s["energy"], s["tot"])
         s["relay_out"][...] = s["tot"][pl.ds(pl.multiple_of((halves + 1 - place.odd) * 16, 16), 16), :]
         relay = remote(s["relay_out"], s["relay_in"], s["relay_sems"], (0,), (place.mate, place.part))
         relay.start()
@@ -641,7 +639,6 @@
     result = brick(
         positions,
         species[None],
-        live_count[None],
         neighbors,
         neighbor_mask,
         send_lo[None],

time: 31 us -> 29.7 us (0.958)
  between operations: 1.29 us -> 0.64 us
  Pallas kernels: 29.5 us -> 28.9 us
    pallas_call x1, Pallas kernels: 28.2 us -> 27.6 us  [brick(): pl.pallas_call(kernel, out_shape=jax.ShapeDtypeStruct((16, LANES), F32),...]
where the time goes in v4:
time: 29.7 us; the launch traced here: 29.5 us
  Pallas kernels  28.9 us (97%)
  between operations  0.64 us (2%)
    pallas_call x1, Pallas kernels, brick(): pl.pallas_call(kernel, out_shape=jax.ShapeDtypeStruct((16, LANES), F32),...  27.6 us
    pallas_call x1, Pallas kernels, split(): pl.pallas_call(kernel, out_shape=tuple((jax.ShapeDtypeStruct((n, share),...  1.3 us

profile of v4, /device:TPU:6, one launch (start us, length us, event | category | flops | bytes accessed | tf_op | source)
XLA Modules:
  0.0 29.5 jit_solution(8856674471477632612)
XLA Ops:
  0.6 27.6 %brick.1.result_ref = f32[16,128]{1,0:T(8,128)} custom-call(f32[3,256]{1,0:T(4,128)} %refs_0_.1, s32[1,256]{1,0:T(1,128)} %bitcast.7, s32[1,128]{1,0:T(1,128)} %bitcast.8, s32[1,128]{1,0:T(1,128)} %bitcast.9, s32[64,256]{1,0:T(8,128)} %refs_4_.1, s32[64,256]{1,0:T(8,128)} %refs_5_.1, f32[20,128]{1,0:T(8,128)} %bitcast.6, bf16[2560,768]{1,0:T(8,128)(2,1)} %refs_7_.1, ...), custom_call_target="tpu_custom_call" | custom-call | tf_op jit(solution)/shard_map/brick/pallas_call | solution.py:605
  28.2 1.3 %split.1 = (f32[3,32]{1,0:T(4,128)}, f32[1,32]{1,0:T(1,128)}, f32[1,32]{1,0:T(1,128)}, f32[6,32]{1,0:T(8,128)}) custom-call(f32[16,128]{1,0:T(8,128)} %brick.1.result_ref), custom_call_target="tpu_custom_call" | custom-call | tf_op jit(solution)/shard_map/split/pallas_call | solution.py:626

commit v5 on v4

--- a/solution.py
+++ b/solution.py
@@ -388,19 +388,24 @@
         def signal(device):
             pl.semaphore_signal(barrier, inc=1, device_id=device, device_id_type=MESH)
 
-        signal((self.mate, self.part))
-
         @pl.when(self.exists)
         def _():
-            for other in self.others:
-                signal((self.cross, other))
-
+            signal((self.cross, self.part))
+
+        signal((self.mate, self.part))
         for other in self.others[1:]:
             signal((self.brick, other))
 
     def met(self):
         barrier = pltpu.get_barrier_semaphore()
-        pl.semaphore_wait(barrier, jnp.where(self.exists, 2 * self.parts, self.parts))
+        pl.semaphore_wait(barrier, jnp.where(self.exists, self.parts + 1, self.parts))
+
+    def tell(self, semaphore):
+        for other in self.others[1:]:
+            pl.semaphore_signal(semaphore, inc=1, device_id=(self.brick, other), device_id_type=MESH)
+
+    def told(self, semaphore):
+        pl.semaphore_wait(semaphore, self.parts - 1)
 
 
 def halo_pick(pos_ref, species_ref, send_refs, table_ref, face_ref):
@@ -466,6 +471,7 @@
         vec_sems=pltpu.SemaphoreType.DMA((2, parts)),
         tot_sems=pltpu.SemaphoreType.DMA((2, parts)),
         cross_sems=pltpu.SemaphoreType.DMA((2, parts)),
+        ready=pltpu.SemaphoreType.REGULAR,
         load_sems=pltpu.SemaphoreType.DMA((len(inputs),)),
     )
     keys = list(names)
@@ -490,11 +496,13 @@
         place.met()
         near = remote(s["face"].at[1 - place.odd], s["rim"].at[0], s["halo_sems"], (0,), (place.mate, place.part))
         far = remote(s["face"].at[place.odd], s["rim"].at[1], s["halo_sems"], (1,), (place.cross, place.part))
-        near.start()
 
         @pl.when(place.exists)
         def _():
             far.start()
+
+        near.start()
+        place.tell(s["ready"])
 
         @pl.when(jnp.logical_not(place.exists))
         def _():
@@ -547,6 +555,8 @@
             remote(s["cross_out"], s["cross_in"].at[j], s["cross_sems"], (j,), (place.cross, other))
             for j, other in enumerate(place.others)
         ]
+
+        place.told(s["ready"])
 
         @pl.when(place.exists)
         def _():

time: 29.7 us -> 28.7 us (0.966)
  Pallas kernels: 28.9 us -> 27.9 us
    pallas_call x1, Pallas kernels: 27.6 us -> 26.6 us  [brick(): pl.pallas_call(kernel, out_shape=jax.ShapeDtypeStruct((16, LANES), F32),...]
where the time goes in v5:
time: 28.7 us; the launch traced here: 28.5 us
  Pallas kernels  27.9 us (97%)
  between operations  0.64 us (2%)
    pallas_call x1, Pallas kernels, brick(): pl.pallas_call(kernel, out_shape=jax.ShapeDtypeStruct((16, LANES), F32),...  26.6 us
    pallas_call x1, Pallas kernels, split(): pl.pallas_call(kernel, out_shape=tuple((jax.ShapeDtypeStruct((n, share),...  1.3 us

profile of v5, /device:TPU:6, one launch (start us, length us, event | category | flops | bytes accessed | tf_op | source)
XLA Modules:
  0.0 28.5 jit_solution(2128169860013580586)
XLA Ops:
  0.6 26.6 %brick.1.result_ref = f32[16,128]{1,0:T(8,128)} custom-call(f32[3,256]{1,0:T(4,128)} %refs_0_.1, s32[1,256]{1,0:T(1,128)} %bitcast.7, s32[1,128]{1,0:T(1,128)} %bitcast.8, s32[1,128]{1,0:T(1,128)} %bitcast.9, s32[64,256]{1,0:T(8,128)} %refs_4_.1, s32[64,256]{1,0:T(8,128)} %refs_5_.1, f32[20,128]{1,0:T(8,128)} %bitcast.6, bf16[2560,768]{1,0:T(8,128)(2,1)} %refs_7_.1, ...), custom_call_target="tpu_custom_call" | custom-call | tf_op jit(solution)/shard_map/brick/pallas_call | solution.py:615
  27.2 1.3 %split.1 = (f32[3,32]{1,0:T(4,128)}, f32[1,32]{1,0:T(1,128)}, f32[1,32]{1,0:T(1,128)}, f32[6,32]{1,0:T(8,128)}) custom-call(f32[16,128]{1,0:T(8,128)} %brick.1.result_ref), custom_call_target="tpu_custom_call" | custom-call | tf_op jit(solution)/shard_map/split/pallas_call | solution.py:636

commit v6 on v5

--- a/solution.py
+++ b/solution.py
@@ -168,18 +168,18 @@
         ).astype(BF16)
 
 
-def kernel_sums(desc_ref, sparse_ref, scale_ref, factor_ref, grad_ref, vec_ref, energy_ref):
+def kernel_sums(desc_ref, sparse_ref, scale_ref, grad_ref, kernel_ref, row_ref):
     raw = sparse_ref[...]
     projection = lax.dot_general(desc_ref[...], raw, NT, preferred_element_type=F32)
     coefficient = projection * scale_ref[1:2, :]
-    kernel = projection * projection * scale_ref[0:1, :]
+    kernel = (projection * projection * scale_ref[0:1, :]).astype(BF16)
     energy_terms = coefficient * projection
     energy = energy_terms[:, :LANES]
     for j in range(1, raw.shape[0] // LANES):
         energy = energy + energy_terms[:, j * LANES : (j + 1) * LANES]
-    energy_ref[...] = energy
     grad_ref[...] = jnp.dot(coefficient.astype(BF16), raw, preferred_element_type=F32)
-    vec_ref[...] = jnp.dot(kernel.astype(BF16), factor_ref[...], preferred_element_type=F32)
+    kernel_ref[...] = kernel
+    row_ref[...] = energy
 
 
 def moment_grads(grad_ref, desc_ref, eye_ref, gd_ref, gt_ref, mc_ref, rinv_ref, g_ref):
@@ -262,7 +262,7 @@
     lax.fori_loop(0, halves * blocks, step, 0)
 
 
-def scatter(nb_ref, hot_ref, t_ref, own_ref, energy_ref, tot_ref, unroll=32):
+def scatter(nb_ref, hot_ref, t_ref, tot_ref, unroll=32):
     count, own = nb_ref.shape
     halves = own // LANES
     tables = tot_ref.shape[0] // 16
@@ -287,24 +287,30 @@
         )
 
     total = lax.fori_loop(0, count // unroll, step, jnp.zeros((groups * 8 + 16, LOW), F32))
-    energies = 0.5 * lax.dot_general(
-        jnp.ones((16, LANES), F32), energy_ref[...], NT, precision=lax.Precision.HIGHEST, preferred_element_type=F32
-    )
     row = lax.broadcasted_iota(jnp.int32, (8, LANES), 0)
-    for t in range(tables):
-        main = jnp.concatenate([total[(t * per + g) * 8 : (t * per + g + 1) * 8] for g in range(per)], axis=1)
+    for t in reversed(range(tables)):
+        tot_ref[t * 16 : t * 16 + 8, :] = jnp.concatenate(
+            [total[(t * per + g) * 8 : (t * per + g + 1) * 8] for g in range(per)], axis=1
+        )
         last = jnp.concatenate(
             [total[groups * 8 + t * per + g : groups * 8 + t * per + g + 1] for g in range(per)], axis=1
         )
-        rest = jnp.where(row == 0, last, 0.0)
-        if t < halves:
-            mine = own_ref[t, pl.ds(0, 16, stride=8), :]
-            for j in range(1, 8):
-                mine = mine + own_ref[t, pl.ds(j, 16, stride=8), :]
-            main = main + mine[:8]
-            rest = rest + jnp.where(row == 1, energies[:8, t * LANES : (t + 1) * LANES], mine[8:])
-        tot_ref[t * 16 : t * 16 + 8, :] = main
-        tot_ref[t * 16 + 8 : t * 16 + 16, :] = rest
+        tot_ref[t * 16 + 8 : t * 16 + 16, :] = jnp.where(row == 0, last, 0.0)
+
+
+def own_terms(own_ref, row_ref, h):
+    mine = own_ref[h, pl.ds(0, 16, stride=8), :]
+    for j in range(1, 8):
+        mine = mine + own_ref[h, pl.ds(j, 16, stride=8), :]
+    row = lax.broadcasted_iota(jnp.int32, (16, LANES), 0)
+    energies = 0.5 * lax.dot_general(
+        jnp.ones((8, LANES), F32),
+        row_ref[h * LANES : (h + 1) * LANES, :],
+        NT,
+        precision=lax.Precision.HIGHEST,
+        preferred_element_type=F32,
+    )
+    return jnp.where(row == 9, energies[0:1], mine)
 
 
 def one_hots(nb_ref, hot_ref):
@@ -348,7 +354,8 @@
         eye=pltpu.VMEM((2 * K * K, K * K), BF16),
         scale=pltpu.VMEM((8, sparse), F32),
         grad=pltpu.VMEM((own, depth), F32),
-        energy=pltpu.VMEM((own, LANES), F32),
+        row=pltpu.VMEM((own, LANES), F32),
+        kernel=pltpu.VMEM((own, sparse), BF16),
         gd=pltpu.VMEM((own, depth), BF16),
         gt=pltpu.VMEM((halves, 3, 2 * K * K, LANES), F32),
         g=pltpu.VMEM((halves * 20, K, LANES), F32),
@@ -435,8 +442,7 @@
     high = ghosts.astype(BF16)
     low = (ghosts - high.astype(F32)).astype(BF16)
     both = lax.dot_general(jnp.concatenate([high, low], axis=0), slots, NT, preferred_element_type=F32)
-    row = lax.broadcasted_iota(jnp.int32, (16, both.shape[1]), 0)
-    return jnp.where(row < 9, both[:16] + both[16:], 0.0)
+    return both[:16] + both[16:]
 
 
 def slots_of(send, first, count):
@@ -456,7 +462,6 @@
         table=pltpu.VMEM((8, tables * LANES), F32),
         face=pltpu.VMEM((2, 8, LANES), F32),
         rim=pltpu.VMEM((2, 8, LANES), F32),
-        vec=pltpu.VMEM((own, rank), F32),
         tot=pltpu.VMEM((tables * 16, LANES), F32),
         vec_out=pltpu.VMEM((own, rank), BF16),
         vec_in=pltpu.VMEM((parts, share, rank), BF16),
@@ -529,8 +534,27 @@
         )
         moments(s["off"], s["w"], s["r"], s["acc"], s["m"], s["mc"])
         descriptors(s["m"], s["mc"], s["d"], s["rinv"], s["desc"], s["plain"])
-        kernel_sums(s["desc"], sparse_ref, s["scale"], factor_ref, s["grad"], s["vec"], s["energy"])
-        s["vec_out"][...] = s["vec"][...].astype(BF16)
+        kernel_sums(s["desc"], sparse_ref, s["scale"], s["grad"], s["kernel"], s["row"])
+        moment_grads(s["grad"], s["desc"], s["eye"], s["gd"], s["gt"], s["mc"], s["rinv"], s["g"])
+        pair_terms(s["off"], s["kind"], s["r"], s["g"], s["t"], s["own"])
+        scatter(nb_ref, s["hot"], s["t"], s["tot"])
+        s["cross_out"][...] = s["tot"][pl.ds(pl.multiple_of((halves + place.odd) * 16, 16), 16), :].astype(BF16)
+        crossing = [
+            remote(s["cross_out"], s["cross_in"].at[j], s["cross_sems"], (j,), (place.cross, other))
+            for j, other in enumerate(place.others)
+        ]
+
+        place.told(s["ready"])
+
+        @pl.when(place.exists)
+        def _():
+            for copy in crossing[::-1]:
+                copy.start()
+
+        s["relay_out"][...] = s["tot"][pl.ds(pl.multiple_of((halves + 1 - place.odd) * 16, 16), 16), :]
+        relay = remote(s["relay_out"], s["relay_in"], s["relay_sems"], (0,), (place.mate, place.part))
+        relay.start()
+        s["vec_out"][...] = jnp.dot(s["kernel"][...], factor_ref[...], preferred_element_type=F32).astype(BF16)
         vectors = [
             remote(
                 s["vec_out"].at[pl.ds(pl.multiple_of(other * share, share), share)],
@@ -544,34 +568,16 @@
         ]
         for copy in vectors:
             copy.start()
-        moment_grads(s["grad"], s["desc"], s["eye"], s["gd"], s["gt"], s["mc"], s["rinv"], s["g"])
-        pair_terms(s["off"], s["kind"], s["r"], s["g"], s["t"], s["own"])
-        scatter(nb_ref, s["hot"], s["t"], s["own"], s["energy"], s["tot"])
-        s["relay_out"][...] = s["tot"][pl.ds(pl.multiple_of((halves + 1 - place.odd) * 16, 16), 16), :]
-        relay = remote(s["relay_out"], s["relay_in"], s["relay_sems"], (0,), (place.mate, place.part))
-        relay.start()
-        s["cross_out"][...] = s["tot"][pl.ds(pl.multiple_of((halves + place.odd) * 16, 16), 16), :].astype(BF16)
-        crossing = [
-            remote(s["cross_out"], s["cross_in"].at[j], s["cross_sems"], (j,), (place.cross, other))
-            for j, other in enumerate(place.others)
-        ]
-
-        place.told(s["ready"])
-
-        @pl.when(place.exists)
-        def _():
-            for copy in crossing[::-1]:
-                copy.start()
-
         odd = place.odd == 1
         near_send = jnp.where(odd, lo_ref[...], hi_ref[...])
         far_send = jnp.where(odd, hi_ref[...], lo_ref[...])
         near_slots = slots_of(near_send, 0, own)
+        mine = [s["tot"][h * 16 : (h + 1) * 16, :] + own_terms(s["own"], s["row"], h) for h in range(halves)]
         relay.wait()
         near_part = deliver(s["relay_in"][...], near_slots)
         for h in range(halves):
             s["tot_out"][h] = (
-                s["tot"][h * 16 : (h + 1) * 16, :] + near_part[:, h * LANES : (h + 1) * LANES]
+                mine[h] + near_part[:, h * LANES : (h + 1) * LANES]
             ).astype(BF16)
         totals = [
             remote(

time: 28.7 us -> 28.5 us (level)
  no operation moved by 1% of the time
where the time goes in v6:
time: 28.5 us; the launch traced here: 28.3 us
  Pallas kernels  27.7 us (97%)
  between operations  0.64 us (2%)
    pallas_call x1, Pallas kernels, brick(): pl.pallas_call(kernel, out_shape=jax.ShapeDtypeStruct((16, LANES), F32),...  26.4 us
    pallas_call x1, Pallas kernels, split(): pl.pallas_call(kernel, out_shape=tuple((jax.ShapeDtypeStruct((n, share),...  1.3 us

profile of v6, /device:TPU:6, one launch (start us, length us, event | category | flops | bytes accessed | tf_op | source)
XLA Modules:
  0.0 28.3 jit_solution(5879056709516291613)
XLA Ops:
  0.6 26.4 %brick.1.result_ref = f32[16,128]{1,0:T(8,128)} custom-call(f32[3,256]{1,0:T(4,128)} %refs_0_.1, s32[1,256]{1,0:T(1,128)} %bitcast.7, s32[1,128]{1,0:T(1,128)} %bitcast.8, s32[1,128]{1,0:T(1,128)} %bitcast.9, s32[64,256]{1,0:T(8,128)} %refs_4_.1, s32[64,256]{1,0:T(8,128)} %refs_5_.1, f32[20,128]{1,0:T(8,128)} %bitcast.6, bf16[2560,768]{1,0:T(8,128)(2,1)} %refs_7_.1, ...), custom_call_target="tpu_custom_call" | custom-call | tf_op jit(solution)/shard_map/brick/pallas_call | solution.py:621
  27.0 1.3 %split.1 = (f32[3,32]{1,0:T(4,128)}, f32[1,32]{1,0:T(1,128)}, f32[1,32]{1,0:T(1,128)}, f32[6,32]{1,0:T(8,128)}) custom-call(f32[16,128]{1,0:T(8,128)} %brick.1.result_ref), custom_call_target="tpu_custom_call" | custom-call | tf_op jit(solution)/shard_map/split/pallas_call | solution.py:642

commit v7 on v6

--- a/solution.py
+++ b/solution.py
@@ -158,7 +158,7 @@
             fresh.append(total)
         return tuple(fresh)
 
-    squares = lax.fori_loop(0, K, step, (jnp.zeros((K, LANES), F32),) * halves, unroll=8)
+    squares = lax.fori_loop(0, K, step, (jnp.zeros((K, LANES), F32),) * halves, unroll=16)
     for h in range(halves):
         rinv = lax.rsqrt(jnp.sum(squares[h], axis=0, keepdims=True) + EPS)
         rinv_ref[h] = jnp.broadcast_to(rinv, (8, LANES))
@@ -209,7 +209,7 @@
                 g_ref[i * 10 + m] = total[m] * rinv
         return 0
 
-    lax.fori_loop(0, halves * 2, step, 0)
+    lax.fori_loop(0, halves * 2, step, 0, unroll=2)
 
 
 def pair_terms(off_ref, kind_ref, r_ref, g_ref, t_ref, own_ref, group=2):
@@ -262,13 +262,15 @@
     lax.fori_loop(0, halves * blocks, step, 0)
 
 
-def scatter(nb_ref, hot_ref, t_ref, tot_ref, unroll=32):
+def scatter(nb_ref, hot_ref, t_ref, tot_ref, picks, unroll=32):
     count, own = nb_ref.shape
     halves = own // LANES
-    tables = tot_ref.shape[0] // 16
-    groups = tables * LANES // LOW
     per = LANES // LOW
+    groups = [table * per + g for table in picks.values() for g in range(per)]
     row = lax.broadcasted_iota(jnp.int32, (8, own), 0)
+    listed = jnp.full((8, own), -1, jnp.int32)
+    for k, group in enumerate(groups):
+        listed = jnp.where(row == k, group, listed)
 
     def step(i, total):
         left, right = [], []
@@ -278,23 +280,22 @@
             high = jnp.broadcast_to(index // LOW, (8, own))
             eight = jnp.concatenate([t_ref[h, pl.ds(n, 8, stride=count), :] for h in range(halves)], axis=1)
             ninth = jnp.concatenate([t_ref[h, pl.ds(8 * count + n, 1), :] for h in range(halves)], axis=1)
-            masked = [jnp.where(high == g, eight, 0.0) for g in range(groups)]
-            masked += [jnp.where(high == row, ninth, 0.0), jnp.zeros((8, own), F32)]
+            masked = [jnp.where(high == group, eight, 0.0) for group in groups]
+            masked += [jnp.where(high == listed, ninth, 0.0), jnp.zeros((8, own), F32)]
             left.append(jnp.concatenate(masked, axis=0).astype(BF16))
             right.append(hot_ref[n])
         return total + lax.dot_general(
             jnp.concatenate(left, axis=1), jnp.concatenate(right, axis=1), NT, preferred_element_type=F32
         )
 
-    total = lax.fori_loop(0, count // unroll, step, jnp.zeros((groups * 8 + 16, LOW), F32))
+    size = len(groups) * 8
+    total = lax.fori_loop(0, count // unroll, step, jnp.zeros((size + 16, LOW), F32))
     row = lax.broadcasted_iota(jnp.int32, (8, LANES), 0)
-    for t in reversed(range(tables)):
+    for k, t in enumerate(picks):
         tot_ref[t * 16 : t * 16 + 8, :] = jnp.concatenate(
-            [total[(t * per + g) * 8 : (t * per + g + 1) * 8] for g in range(per)], axis=1
+            [total[(k * per + g) * 8 : (k * per + g + 1) * 8] for g in range(per)], axis=1
         )
-        last = jnp.concatenate(
-            [total[groups * 8 + t * per + g : groups * 8 + t * per + g + 1] for g in range(per)], axis=1
-        )
+        last = jnp.concatenate([total[size + k * per + g : size + k * per + g + 1] for g in range(per)], axis=1)
         tot_ref[t * 16 + 8 : t * 16 + 16, :] = jnp.where(row == 0, last, 0.0)
 
 
@@ -537,8 +538,8 @@
         kernel_sums(s["desc"], sparse_ref, s["scale"], s["grad"], s["kernel"], s["row"])
         moment_grads(s["grad"], s["desc"], s["eye"], s["gd"], s["gt"], s["mc"], s["rinv"], s["g"])
         pair_terms(s["off"], s["kind"], s["r"], s["g"], s["t"], s["own"])
-        scatter(nb_ref, s["hot"], s["t"], s["tot"])
-        s["cross_out"][...] = s["tot"][pl.ds(pl.multiple_of((halves + place.odd) * 16, 16), 16), :].astype(BF16)
+        scatter(nb_ref, s["hot"], s["t"], s["tot"], {halves + 1: halves + place.odd, halves: halves + 1 - place.odd})
+        s["cross_out"][...] = s["tot"][(halves + 1) * 16 :, :].astype(BF16)
         crossing = [
             remote(s["cross_out"], s["cross_in"].at[j], s["cross_sems"], (j,), (place.cross, other))
             for j, other in enumerate(place.others)
@@ -548,12 +549,13 @@
 
         @pl.when(place.exists)
         def _():
-            for copy in crossing[::-1]:
-                copy.start()
-
-        s["relay_out"][...] = s["tot"][pl.ds(pl.multiple_of((halves + 1 - place.odd) * 16, 16), 16), :]
+            for j in sorted(range(parts), key=lambda j: -min(j, parts - j)):
+                crossing[j].start()
+
+        s["relay_out"][...] = s["tot"][halves * 16 : (halves + 1) * 16, :]
         relay = remote(s["relay_out"], s["relay_in"], s["relay_sems"], (0,), (place.mate, place.part))
         relay.start()
+        scatter(nb_ref, s["hot"], s["t"], s["tot"], {h: h for h in range(halves)})
         s["vec_out"][...] = jnp.dot(s["kernel"][...], factor_ref[...], preferred_element_type=F32).astype(BF16)
         vectors = [
             remote(

time: 28.5 us -> 28.2 us (0.989)
  Pallas kernels: 27.7 us -> 27.4 us
    pallas_call x1, Pallas kernels: 26.4 us -> 26.1 us  [brick(): pl.pallas_call(kernel, out_shape=jax.ShapeDtypeStruct((16, LANES), F32),...]
where the time goes in v7:
time: 28.2 us; the launch traced here: 28 us
  Pallas kernels  27.4 us (97%)
  between operations  0.64 us (2%)
    pallas_call x1, Pallas kernels, brick(): pl.pallas_call(kernel, out_shape=jax.ShapeDtypeStruct((16, LANES), F32),...  26.1 us
    pallas_call x1, Pallas kernels, split(): pl.pallas_call(kernel, out_shape=tuple((jax.ShapeDtypeStruct((n, share),...  1.3 us

profile of v7, /device:TPU:6, one launch (start us, length us, event | category | flops | bytes accessed | tf_op | source)
XLA Modules:
  0.0 28.0 jit_solution(7333761487621994472)
XLA Ops:
  0.6 26.1 %brick.1.result_ref = f32[16,128]{1,0:T(8,128)} custom-call(f32[3,256]{1,0:T(4,128)} %refs_0_.1, s32[1,256]{1,0:T(1,128)} %bitcast.7, s32[1,128]{1,0:T(1,128)} %bitcast.8, s32[1,128]{1,0:T(1,128)} %bitcast.9, s32[64,256]{1,0:T(8,128)} %refs_4_.1, s32[64,256]{1,0:T(8,128)} %refs_5_.1, f32[20,128]{1,0:T(8,128)} %bitcast.6, bf16[2560,768]{1,0:T(8,128)(2,1)} %refs_7_.1, ...), custom_call_target="tpu_custom_call" | custom-call | tf_op jit(solution)/shard_map/brick/pallas_call | solution.py:623
  26.7 1.3 %split.1 = (f32[3,32]{1,0:T(4,128)}, f32[1,32]{1,0:T(1,128)}, f32[1,32]{1,0:T(1,128)}, f32[6,32]{1,0:T(8,128)}) custom-call(f32[16,128]{1,0:T(8,128)} %brick.1.result_ref), custom_call_target="tpu_custom_call" | custom-call | tf_op jit(solution)/shard_map/split/pallas_call | solution.py:644

commit v8 on v7

--- a/solution.py
+++ b/solution.py
@@ -346,7 +346,7 @@
         w=pltpu.VMEM((halves, SPECIES - 1, count, LANES), F32),
         kind=pltpu.VMEM((halves, count, LANES), jnp.int32),
         r=pltpu.VMEM((halves, len(RATES), count, LANES), F32),
-        acc=pltpu.VMEM((halves * 20, K * 8, LANES), F32),
+        acc=pltpu.VMEM((halves * 20, K * 8 + 8, LANES), F32),
         m=pltpu.VMEM((halves * 20, K, LANES), F32),
         mc=pltpu.VMEM((halves * 20, K, LANES), F32),
         d=pltpu.VMEM((halves, depth, LANES), F32),
@@ -361,7 +361,7 @@
         gt=pltpu.VMEM((halves, 3, 2 * K * K, LANES), F32),
         g=pltpu.VMEM((halves * 20, K, LANES), F32),
         t=pltpu.VMEM((halves, 9 * count, LANES), F32),
-        own=pltpu.VMEM((halves, 16 * 8, LANES), F32),
+        own=pltpu.VMEM((halves, 16 * 8 + 8, LANES), F32),
         hot=pltpu.VMEM((count, LOW, own), BF16),
     )
 

time: 28.2 us -> 28.1 us (level)
  no operation moved by 1% of the time
where the time goes in v8:
time: 28.1 us; the launch traced here: 27.9 us
  Pallas kernels  27.3 us (97%)
  between operations  0.64 us (2%)
    pallas_call x1, Pallas kernels, brick(): pl.pallas_call(kernel, out_shape=jax.ShapeDtypeStruct((16, LANES), F32),...  26 us
    pallas_call x1, Pallas kernels, split(): pl.pallas_call(kernel, out_shape=tuple((jax.ShapeDtypeStruct((n, share),...  1.3 us

profile of v8, /device:TPU:6, one launch (start us, length us, event | category | flops | bytes accessed | tf_op | source)
XLA Modules:
  0.0 27.9 jit_solution(8645740712967751860)
XLA Ops:
  0.6 26.0 %brick.1.result_ref = f32[16,128]{1,0:T(8,128)} custom-call(f32[3,256]{1,0:T(4,128)} %refs_0_.1, s32[1,256]{1,0:T(1,128)} %bitcast.7, s32[1,128]{1,0:T(1,128)} %bitcast.8, s32[1,128]{1,0:T(1,128)} %bitcast.9, s32[64,256]{1,0:T(8,128)} %refs_4_.1, s32[64,256]{1,0:T(8,128)} %refs_5_.1, f32[20,128]{1,0:T(8,128)} %bitcast.6, bf16[2560,768]{1,0:T(8,128)(2,1)} %refs_7_.1, ...), custom_call_target="tpu_custom_call" | custom-call | tf_op jit(solution)/shard_map/brick/pallas_call | solution.py:623
  26.6 1.3 %split.1 = (f32[3,32]{1,0:T(4,128)}, f32[1,32]{1,0:T(1,128)}, f32[1,32]{1,0:T(1,128)}, f32[6,32]{1,0:T(8,128)}) custom-call(f32[16,128]{1,0:T(8,128)} %brick.1.result_ref), custom_call_target="tpu_custom_call" | custom-call | tf_op jit(solution)/shard_map/split/pallas_call | solution.py:644
